TPU v7x, 32 devices: a whole 2x2x4 slice. The times are simulated.
32 devices in a mesh: dp: 8 (over y, x, core), expert: 4 (over z).
Axes of the slice: x: 2, y: 2, z: 4, core: 2. Of those that a mesh axis runs over, the one named last changes fastest.
Arguments:
- tokens: bfloat16 [16384, 768], P(('dp', 'expert')), may hold values from -6 to 6
- query_weight: bfloat16 [768, 768], P('dp'), may hold values from -0.21875 to 0.21875
- key_weight: bfloat16 [768, 768], P('dp'), may hold values from -0.21875 to 0.21875
- value_weight: bfloat16 [768, 768], P('dp'), may hold values from -0.21875 to 0.21875
- project_weight: bfloat16 [768, 768], P('dp'), may hold values from -0.875 to 0.875
- router_weight: bfloat16 [768, 8], P('dp'), may hold values from -0.21875 to 0.21875
- prenorm_gain: bfloat16 [768], P('dp'), may hold values from 0.5 to 1.5
- midnorm_gain: bfloat16 [768], P('dp'), may hold values from 0.5 to 1.5
- bias_table: bfloat16 [32, 12], P('dp'), may hold values from -5 to 5
- up_weight: bfloat16 [8, 768, 3072], P('expert', None, 'dp'), may hold values from -0.21875 to 0.21875
- down_weight: bfloat16 [8, 3072, 768], P('expert', 'dp'), may hold values from -0.109375 to 0.109375
- routes: int32 [16384, 2], P(('dp', 'expert')), may hold values from 0 to 7, all different within a row; in each aligned block of 512 rows (0 to 511, 512 to 1023, ...) at most 192 rows name the same one
- bucket_index: int32 [512], replicated, may hold values from 0 to 31
- cotangent: bfloat16 [16384, 768], P(('dp', 'expert')), may hold values from -6 to 6
Outputs:
- layer_out: bfloat16 [16384, 768], P(('dp', 'expert'))
- inputs_grad: bfloat16 [16384, 768], P(('dp', 'expert'))
- query_grad: float32 [768, 768], P('dp')
- key_grad: float32 [768, 768], P('dp')
- value_grad: float32 [768, 768], P('dp')
- project_grad: float32 [768, 768], P('dp')
- router_grad: float32 [768, 8], P('dp')
- prenorm_grad: float32 [768], P('dp')
- midnorm_grad: float32 [768], P('dp')
- table_grad: float32 [32, 12], P('dp')
- up_grad: float32 [8, 768, 3072], P('expert', None, 'dp')
- down_grad: float32 [8, 3072, 768], P('expert', 'dp')
Inputs may be any that keep to these rules, and one draw needn't show every extreme that they name: `routes`: among the 512 rows of one sequence no expert is named more than 192 times, and in every draw some expert is named exactly 192 times in some sequence; the two experts of a token differ.
All inputs are finite; a program needn't handle non-finite values.
Results may differ from a plain program's by a relative error of at most 0.019.
Values may be sent and summed in bfloat16 or wider, within the bound.
A program may use at most 256 MiB of HBM per device.

v0:
```python
from functools import partial

import jax
import jax.numpy as jnp
from jax import lax
from jax.sharding import PartitionSpec as P

HEADS = 12
HEAD_DIM = 64


EPSILON = 1e-06
NEGATIVE = -1e30


def norm_rows(values, gain):
    return values * lax.rsqrt(jnp.mean(values * values, axis=-1, keepdims=True) + EPSILON) * gain


def product(left, right):
    return jnp.dot(left, right, preferred_element_type=jnp.float32)


def product_tn(left, right):
    return lax.dot_general(
        left, right, (((0,), (0,)), ((), ())), preferred_element_type=jnp.float32
    )


def product_nt(left, right):
    return lax.dot_general(
        left, right, (((1,), (1,)), ((), ())), preferred_element_type=jnp.float32
    )


def slot_places(route_seq, capacity, experts_all):
    count = route_seq.shape[0] * route_seq.shape[1]
    flat = route_seq.reshape(count)
    onehot = (flat[:, None] == jnp.arange(experts_all, dtype=jnp.int32)[None, :]).astype(
        jnp.bfloat16
    )
    positions = jnp.arange(count, dtype=jnp.int32)
    earlier_mask = (positions[:, None] > positions[None, :]).astype(jnp.bfloat16)
    before = product(earlier_mask, onehot)
    slot = jnp.sum(before * onehot.astype(jnp.float32), axis=1).astype(jnp.int32)
    return flat * capacity + slot


def offset_line(by_offset):
    flipped = by_offset.T
    heads, seq_len = flipped.shape
    blank = jnp.zeros((heads, seq_len), flipped.dtype)
    return jnp.concatenate([flipped[:, :1], blank, flipped[:, :0:-1]], axis=1)


def bias_block(offset_w, start, block):
    heads, period = offset_w.shape
    seq_len = period // 2
    rolled = jnp.roll(offset_w, start, axis=1)
    tiled = jnp.tile(rolled, (1, block + 1))[:, : block * (period - 1)]
    return tiled.reshape(heads, block, period - 1)[:, :, :seq_len].astype(jnp.float32)


def diagonal_sums(grad_scores, start):
    heads, block, seq_len = grad_scores.shape
    period = 2 * seq_len
    widened = jnp.pad(grad_scores, ((0, 0), (0, 0), (0, seq_len - 1)))
    flat = jnp.pad(widened.reshape(heads, block * (period - 1)), ((0, 0), (0, block)))
    summed = jnp.sum(flat.reshape(heads, block, period), axis=1)
    return jnp.roll(summed, -start, axis=1)


def scores_block(query_rows, key, offset_w, start, rows_at, keys_at):
    block = query_rows.shape[1]
    bias = bias_block(offset_w, start, block)
    scores = (
        jnp.einsum("hqd,hkd->hqk", query_rows, key, preferred_element_type=jnp.float32)
        * HEAD_DIM ** (-0.5)
        + bias
    )
    return jnp.where((rows_at[:, None] >= keys_at[None, :])[None], scores, NEGATIVE)


def attend_forward(query, key, value, offset_w):
    seq_len = query.shape[1]
    keys_at = jnp.arange(seq_len, dtype=jnp.int32)
    scores = scores_block(query, key, offset_w, 0, keys_at, keys_at)
    top = jnp.max(scores, axis=-1, keepdims=True)
    total = top + jnp.log(jnp.sum(jnp.exp(scores - top), axis=-1, keepdims=True))
    probs = jnp.exp(scores - total).astype(jnp.bfloat16)
    outputs = jnp.einsum("hqk,hkd->hqd", probs, value, preferred_element_type=jnp.float32)
    return (outputs, total)


def attend_backward(query, key, value, offset_w, totals, grad_out):
    heads, seq_len, head_dim = query.shape
    scale = HEAD_DIM ** (-0.5)
    keys_at = jnp.arange(seq_len, dtype=jnp.int32)
    scores = scores_block(query, key, offset_w, 0, keys_at, keys_at)
    probs = jnp.exp(scores - totals)
    grad_probs = jnp.einsum("hqd,hkd->hqk", grad_out, value, preferred_element_type=jnp.float32)
    inner = jnp.sum(probs * grad_probs, axis=-1, keepdims=True)
    grad_scores = (probs * (grad_probs - inner)).astype(jnp.bfloat16)
    grad_rows_q = (
        jnp.einsum("hqk,hkd->hqd", grad_scores, key, preferred_element_type=jnp.float32) * scale
    )
    grad_key = (
        jnp.einsum("hqk,hqd->hkd", grad_scores, query, preferred_element_type=jnp.float32) * scale
    )
    grad_value = jnp.einsum(
        "hqk,hqd->hkd", probs.astype(jnp.bfloat16), grad_out, preferred_element_type=jnp.float32
    )
    grad_line = diagonal_sums(grad_scores.astype(jnp.float32), 0)
    grad_distance = jnp.concatenate([grad_line[:, :1], grad_line[:, :seq_len:-1]], axis=1)
    return (grad_rows_q, grad_key, grad_value, grad_distance)


def body(
    tokens,
    query_weight,
    key_weight,
    value_weight,
    project_weight,
    router_weight,
    prenorm_gain,
    midnorm_gain,
    bias_table,
    up_weight,
    down_weight,
    routes,
    bucket_index,
    cotangent,
):
    attention_full = (
        lax.all_gather(query_weight, "dp", axis=0, tiled=True),
        lax.all_gather(key_weight, "dp", axis=0, tiled=True),
        lax.all_gather(value_weight, "dp", axis=0, tiled=True),
        lax.all_gather(project_weight, "dp", axis=0, tiled=True),
        lax.all_gather(router_weight, "dp", axis=0, tiled=True),
        lax.all_gather(prenorm_gain, "dp", axis=0, tiled=True),
        lax.all_gather(midnorm_gain, "dp", axis=0, tiled=True),
        lax.all_gather(bias_table, "dp", axis=0, tiled=True),
    )
    expert_full = (
        lax.all_gather(up_weight, "dp", axis=2, tiled=True),
        lax.all_gather(down_weight, "dp", axis=1, tiled=True),
    )
    (
        query_full,
        key_full,
        value_full,
        project_full,
        router_full,
        gain_first,
        gain_second,
        table_full,
    ) = attention_full
    seq_len, width = tokens.shape
    experts_all = router_weight.shape[1]
    owners = lax.axis_size("expert")
    local_count = up_weight.shape[0]
    capacity = 3 * seq_len // experts_all
    buckets = table_full.shape[0]
    gain_first = gain_first.astype(jnp.float32)
    gain_second = gain_second.astype(jnp.float32)

    def split_heads(values):
        return values.reshape(seq_len, HEADS, HEAD_DIM).transpose(1, 0, 2)

    def join_heads(values):
        return values.transpose(1, 0, 2).reshape(seq_len, width).astype(jnp.bfloat16)

    bucket_hot = (bucket_index[:, None] == jnp.arange(buckets, dtype=jnp.int32)[None, :]).astype(
        jnp.bfloat16
    )
    by_offset = product(bucket_hot, table_full).astype(jnp.bfloat16)
    offset_w = offset_line(by_offset)
    inputs = tokens.astype(jnp.float32)
    normed_low = norm_rows(inputs, gain_first).astype(jnp.bfloat16)
    query = split_heads(product(normed_low, query_full).astype(jnp.bfloat16))
    key = split_heads(product(normed_low, key_full).astype(jnp.bfloat16))
    value = split_heads(product(normed_low, value_full).astype(jnp.bfloat16))
    attended, totals = attend_forward(query, key, value, offset_w)
    merged = join_heads(attended)
    middle = inputs + product(merged, project_full)
    second_low = norm_rows(middle, gain_second).astype(jnp.bfloat16)
    logits = product(second_low, router_full)
    choose = (routes[:, :, None] == jnp.arange(experts_all, dtype=jnp.int32)[None, None, :]).astype(
        jnp.float32
    )
    pair = jnp.sum(choose * logits[:, None, :], axis=-1)
    gates = jax.nn.softmax(pair, axis=-1)
    dest = slot_places(routes, capacity, experts_all)
    placing = (
        jnp.arange(experts_all * capacity, dtype=jnp.int32)[:, None] == dest[None, :]
    ).astype(jnp.bfloat16)
    filled = product(placing, jnp.repeat(second_low, 2, axis=0)).astype(jnp.bfloat16)
    arrived = lax.all_to_all(
        filled.reshape(owners, local_count, capacity, width),
        "expert",
        split_axis=0,
        concat_axis=0,
        tiled=True,
    )
    hidden_list = []
    reply_list = []
    for index in range(local_count):
        rows = arrived[:, index].reshape(owners * capacity, width)
        hidden = product(rows, expert_full[0][index])
        active = jax.nn.gelu(hidden, approximate=False).astype(jnp.bfloat16)
        reply_list.append(
            product(active, expert_full[1][index])
            .astype(jnp.bfloat16)
            .reshape(owners, capacity, width)
        )
        hidden_list.append(hidden)
    returned = lax.all_to_all(
        jnp.stack(reply_list, 1), "expert", split_axis=0, concat_axis=0, tiled=True
    ).reshape(experts_all * capacity, width)
    picked = product_tn(placing, returned).reshape(seq_len, 2, width)
    layer_out = middle + jnp.sum(gates[:, :, None] * picked, axis=1)
    query_back, key_back, value_back, project_back, router_back = (
        lax.all_gather(query_weight, "dp", axis=0, tiled=True),
        lax.all_gather(key_weight, "dp", axis=0, tiled=True),
        lax.all_gather(value_weight, "dp", axis=0, tiled=True),
        lax.all_gather(project_weight, "dp", axis=0, tiled=True),
        lax.all_gather(router_weight, "dp", axis=0, tiled=True),
    )
    up_back, down_back = (
        lax.all_gather(up_weight, "dp", axis=2, tiled=True),
        lax.all_gather(down_weight, "dp", axis=1, tiled=True),
    )
    grad_final = cotangent.astype(jnp.float32)
    grad_gates = jnp.sum(picked * grad_final[:, None, :], axis=-1)
    grad_picked = (
        (gates[:, :, None] * grad_final[:, None, :])
        .astype(jnp.bfloat16)
        .reshape(2 * seq_len, width)
    )
    grad_returned = product(placing, grad_picked).astype(jnp.bfloat16)
    grad_replies = lax.all_to_all(
        grad_returned.reshape(owners, local_count, capacity, width),
        "expert",
        split_axis=0,
        concat_axis=0,
        tiled=True,
    )
    grad_rows_list = []
    grad_up_list = []
    grad_down_list = []
    for index in range(local_count):
        rows = arrived[:, index].reshape(owners * capacity, width)
        grad_reply = grad_replies[:, index].reshape(owners * capacity, width)
        active, gelu_pull = jax.vjp(partial(jax.nn.gelu, approximate=False), hidden_list[index])
        grad_down_list.append(product_tn(active.astype(jnp.bfloat16), grad_reply))
        grad_active = product_nt(grad_reply, down_back[index])
        grad_hidden = gelu_pull(grad_active)[0].astype(jnp.bfloat16)
        grad_up_list.append(product_tn(rows, grad_hidden))
        grad_rows_list.append(
            product_nt(grad_hidden, up_back[index])
            .astype(jnp.bfloat16)
            .reshape(owners, capacity, width)
        )
    grad_sent = lax.all_to_all(
        jnp.stack(grad_rows_list, 1), "expert", split_axis=0, concat_axis=0, tiled=True
    ).reshape(experts_all * capacity, width)
    grad_second = jnp.sum(product_tn(placing, grad_sent).reshape(seq_len, 2, width), axis=1)
    grad_pair = gates * (grad_gates - jnp.sum(gates * grad_gates, axis=-1, keepdims=True))
    grad_logits = jnp.sum(grad_pair[:, :, None] * choose, axis=1).astype(jnp.bfloat16)
    grad_router = product_tn(second_low, grad_logits)
    grad_second = grad_second + product_nt(grad_logits, router_back)
    unused_second, second_pull = jax.vjp(norm_rows, middle, gain_second)
    grad_middle_norm, grad_midnorm = second_pull(grad_second)
    grad_middle = grad_final + grad_middle_norm
    grad_branch = grad_middle.astype(jnp.bfloat16)
    grad_project = product_tn(merged, grad_branch)
    grad_merged = split_heads(product_nt(grad_branch, project_back).astype(jnp.bfloat16))
    grad_query, grad_key, grad_value, grad_distance = attend_backward(
        query, key, value, offset_w, totals, grad_merged
    )
    grad_table = jnp.dot(
        bucket_hot.astype(jnp.float32).T,
        grad_distance.T,
        precision=lax.Precision.HIGHEST,
        preferred_element_type=jnp.float32,
    )
    grad_query = join_heads(grad_query)
    grad_key = join_heads(grad_key)
    grad_value = join_heads(grad_value)
    grad_query_w = product_tn(normed_low, grad_query)
    grad_key_w = product_tn(normed_low, grad_key)
    grad_value_w = product_tn(normed_low, grad_value)
    grad_normed = (
        product_nt(grad_query, query_back)
        + product_nt(grad_key, key_back)
        + product_nt(grad_value, value_back)
    )
    unused_first, first_pull = jax.vjp(norm_rows, inputs, gain_first)
    grad_inputs, grad_prenorm = first_pull(grad_normed)
    inputs_grad = (grad_middle + grad_inputs).astype(jnp.bfloat16)
    shares = (
        lax.psum_scatter(
            grad_query_w.astype(jnp.bfloat16), "dp", scatter_dimension=0, tiled=True
        ).astype(jnp.float32),
        lax.psum_scatter(
            grad_key_w.astype(jnp.bfloat16), "dp", scatter_dimension=0, tiled=True
        ).astype(jnp.float32),
        lax.psum_scatter(
            grad_value_w.astype(jnp.bfloat16), "dp", scatter_dimension=0, tiled=True
        ).astype(jnp.float32),
        lax.psum_scatter(
            grad_project.astype(jnp.bfloat16), "dp", scatter_dimension=0, tiled=True
        ).astype(jnp.float32),
        lax.psum_scatter(
            grad_router.astype(jnp.bfloat16), "dp", scatter_dimension=0, tiled=True
        ).astype(jnp.float32),
        lax.psum_scatter(
            grad_prenorm.astype(jnp.bfloat16), "dp", scatter_dimension=0, tiled=True
        ).astype(jnp.float32),
        lax.psum_scatter(
            grad_midnorm.astype(jnp.bfloat16), "dp", scatter_dimension=0, tiled=True
        ).astype(jnp.float32),
        lax.psum_scatter(
            grad_table.astype(jnp.bfloat16), "dp", scatter_dimension=0, tiled=True
        ).astype(jnp.float32),
    )
    totals_all = (
        lax.psum(shares[0].astype(jnp.bfloat16), "expert").astype(jnp.float32),
        lax.psum(shares[1].astype(jnp.bfloat16), "expert").astype(jnp.float32),
        lax.psum(shares[2].astype(jnp.bfloat16), "expert").astype(jnp.float32),
        lax.psum(shares[3].astype(jnp.bfloat16), "expert").astype(jnp.float32),
        lax.psum(shares[4].astype(jnp.bfloat16), "expert").astype(jnp.float32),
        lax.psum(shares[5].astype(jnp.bfloat16), "expert").astype(jnp.float32),
        lax.psum(shares[6].astype(jnp.bfloat16), "expert").astype(jnp.float32),
        lax.psum(shares[7].astype(jnp.bfloat16), "expert").astype(jnp.float32),
    )
    expert_grads = (
        lax.psum_scatter(
            jnp.stack(grad_up_list, 0).astype(jnp.bfloat16), "dp", scatter_dimension=2, tiled=True
        ).astype(jnp.float32),
        lax.psum_scatter(
            jnp.stack(grad_down_list, 0).astype(jnp.bfloat16), "dp", scatter_dimension=1, tiled=True
        ).astype(jnp.float32),
    )
    return (
        layer_out.astype(jnp.bfloat16),
        inputs_grad,
        totals_all[0],
        totals_all[1],
        totals_all[2],
        totals_all[3],
        totals_all[4],
        totals_all[5],
        totals_all[6],
        totals_all[7],
        expert_grads[0],
        expert_grads[1],
    )


def solution(mesh):
    return jax.shard_map(
        body,
        mesh=mesh,
        in_specs=(
            P(("dp", "expert"), None),
            P("dp", None),
            P("dp", None),
            P("dp", None),
            P("dp", None),
            P("dp", None),
            P("dp"),
            P("dp"),
            P("dp", None),
            P("expert", None, "dp"),
            P("expert", "dp", None),
            P(("dp", "expert"), None),
            P(),
            P(("dp", "expert"), None),
        ),
        out_specs=(
            P(("dp", "expert"), None),
            P(("dp", "expert"), None),
            P("dp", None),
            P("dp", None),
            P("dp", None),
            P("dp", None),
            P("dp", None),
            P("dp"),
            P("dp"),
            P("dp", None),
            P("expert", None, "dp"),
            P("expert", "dp", None),
        ),
        check_vma=False,
    )
```

profile of v0, /device:TPU:0, one launch (start us, length us, event | category | flops | bytes accessed | tf_op | source)
XLA Modules:
  0.0 952.7 jit_solution(18323138385997573201)
XLA Ops:
  10.6 10.5 %all-gather = bf16[8,4,12]{2,1,0:T(4,128)(2,1)S(1)} all-gather(bf16[1,4,12]{2,1,0:T(4,128)(2,1)} %bitcast.201), channel_id=1, replica_groups=mesh['dp'=8,'expert'=4] {'dp'}, dimensions={0}, use_global_device_ids=true | all-gather | bytes 864 | tf_op jit(solution)/shard_map/all_gather | solution.py:142
  25.7 13.1 %all-reduce.8 = (bf16[768]{0:T(1024)(128)(2,1)S(1)}, bf16[768]{0:T(1024)(128)(2,1)S(1)}) all-reduce(bf16[768]{0:T(1024)(128)(2,1)S(1)} %dynamic-update-slice, bf16[768]{0:T(1024)(128)(2,1)S(1)} %dynamic-update-slice.1), channel_id=1, replica_groups=mesh['dp'=8,'expert'=4] {'dp'}, use_global_device_ids=true, to_apply=%add.2 | all-reduce | flops 1536 | bytes 6144
  39.3 8.9 all-gather.1
  54.8 6.3 tile.4
  61.1 7.0 pad.25
  68.1 52.2 %copy.114 = bf16[2,8,513,1024]{3,1,2,0:T(8,128)(2,1)S(1)} copy(bf16[2,8,513,1024]{3,2,1,0:T(8,128)(2,1)S(1)} %bitcast.164) | data formatting | bytes 33619968
  120.3 6.7 slice.66
  127.0 44.3 %reshape.290 = bf16[12,512,1023]{2,1,0:T(8,128)(2,1)} reshape(bf16[12,523776]{1,0:T(8,128)(2,1)} %slice.66) | data formatting | bytes 25141248 | tf_op jit(solution)/shard_map/reshape | solution.py:61
  171.3 5.9 slice.67
  177.2 8.7 copy.110
  196.6 5.6 fusion.91
  214.7 6.4 fusion.29
  233.2 5.4 fusion.28
  238.6 42.1 %all-to-all-done.2 = bf16[4,2,192,768]{3,2,1,0:T(8,128)(2,1)S(1)} async-done(((bf16[4,2,192,768]{3,2,1,0:T(8,128)(2,1)}), bf16[4,2,192,768]{3,2,1,0:T(8,128)(2,1)S(1)}, u32[]{:S(2)}, u32[]{:S(2)}) %all-to-all-start.2) | async-done | bytes 2359328 | tf_op jit(solution)/shard_map/all_to_all | solution.py:241
  287.1 52.3 %all-to-all-done = bf16[4,2,192,768]{3,2,1,0:T(8,128)(2,1)} async-done(((bf16[4,2,192,768]{3,2,1,0:T(8,128)(2,1)}), bf16[4,2,192,768]{3,2,1,0:T(8,128)(2,1)}, u32[]{:S(2)}, u32[]{:S(2)}) %all-to-all-start) | async-done | bytes 2359328 | tf_op jit(solution)/shard_map/all_to_all | solution.py:198
  341.3 27.2 %multiply_convert_fusion.1 = (bf16[768,3072]{1,0:T(8,128)(2,1)}, f32[768,3072]{1,0:T(8,128)}, f32[768,3072]{1,0:T(8,128)}) fusion(bf16[768,768]{1,0:T(8,128)(2,1)S(1)} %bitcast.191, bf16[2,768,3072]{2,1,0:T(8,128)(2,1)} %all-gather.17.cloned.1.call-done), kind=kOutput, calls=%fused_computation.16 | convolution fusion | flops 3777232896 | bytes 29491200 | tf_op jit(solution)/shard_map/dot_general | solution.py:21
  368.5 25.7 %multiply_convert_fusion.2 = (bf16[768,3072]{1,0:T(8,128)(2,1)}, f32[768,3072]{1,0:T(8,128)}, f32[768,3072]{1,0:T(8,128)}) fusion(bf16[768,768]{1,0:T(8,128)(2,1)S(1)} %bitcast.189, bf16[2,768,3072]{2,1,0:T(8,128)(2,1)S(1)} %copy-done.55), kind=kOutput, calls=%fused_computation.29 | convolution fusion | flops 3777232896 | bytes 29491200 | tf_op jit(solution)/shard_map/dot_general | solution.py:21
  394.3 7.7 fusion.49
  412.2 10.9 %add_convert_fusion = bf16[768,3072]{1,0:T(8,128)(2,1)S(1)} fusion(f32[768,3072]{1,0:T(8,128)} %get-tuple-element.34, f32[768,3072]{1,0:T(8,128)} %get-tuple-element.47, bf16[768,768]{1,0:T(8,128)(2,1)S(1)} %bitcast.188, bf16[2,3072,768]{2,1,0:T(8,128)(2,1)} %all-gather.19.cloned.1.call-done), kind=kOutput, calls=%fused_computation.14 | convolution fusion | flops 3656908800 | bytes 29491200 | tf_op jit(solution)/shard_map/dot_general | solution.py:31
  423.1 7.9 fusion.50
  431.1 11.2 %add_convert_fusion.1 = bf16[768,3072]{1,0:T(8,128)(2,1)S(1)} fusion(f32[768,3072]{1,0:T(8,128)} %get-tuple-element.32, f32[768,3072]{1,0:T(8,128)} %get-tuple-element.48, bf16[768,768]{1,0:T(8,128)(2,1)S(1)} %bitcast.185, bf16[2,3072,768]{2,1,0:T(8,128)(2,1)} %all-gather.19.cloned.1.call-done), kind=kOutput, calls=%fused_computation.15 | convolution fusion | flops 3656908800 | bytes 29491200 | tf_op jit(solution)/shard_map/dot_general | solution.py:31
  447.9 17.7 %all-to-all-done.1 = bf16[4,2,192,768]{3,2,1,0:T(8,128)(2,1)} async-done(((bf16[4,2,192,768]{3,2,1,0:T(8,128)(2,1)}), bf16[4,2,192,768]{3,2,1,0:T(8,128)(2,1)}, u32[]{:S(2)}, u32[]{:S(2)}) %all-to-all-start.1) | async-done | bytes 2359328 | tf_op jit(solution)/shard_map/all_to_all | solution.py:217
  476.8 7.2 multiply_reduce_fusion.1
  484.1 39.4 %all-to-all-done.3 = bf16[4,2,192,768]{3,2,1,0:T(8,128)(2,1)} async-done(((bf16[4,2,192,768]{3,2,1,0:T(8,128)(2,1)}), bf16[4,2,192,768]{3,2,1,0:T(8,128)(2,1)}, u32[]{:S(2)}, u32[]{:S(2)}) %all-to-all-start.3) | async-done | bytes 2359328 | tf_op jit(solution)/shard_map/all_to_all | solution.py:264
  523.5 5.4 convolution_reduce_fusion
  536.4 6.8 fusion.56
  546.1 9.0 multiply_reduce_fusion
  555.2 9.9 %multiply_convert_fusion = bf16[12,512,512]{1,2,0:T(8,128)(2,1)S(1)} fusion(f32[12,512,512]{1,2,0:T(8,128)} %get-tuple-element.51, f32[12,512,512]{1,2,0:T(8,128)} %copy-done, f32[12,512]{1,0:T(8,128)S(1)} %get-tuple-element.50, f32[12,512]{1,0:T(8,128)S(1)} %copy-done.28), kind=kLoop, calls=%fused_computation.4 | loop fusion | flops 12582912 | bytes 31506432 | tf_op jit(solution)/shard_map/convert_element_type | solution.py:103
  569.8 5.1 multiply_convert_fusion.5
  579.1 8.9 fusion.16
  588.0 23.4 %reduce-scatter.16.cloned.1.call-done = bf16[96,768]{1,0:T(8,128)(2,1)} async-done(((bf16[768,768]{1,0:T(8,128)(2,1)}), bf16[96,768]{1,0:T(8,128)(2,1)}) %reduce-scatter.16.cloned.1.call-update) | async-done | bytes 147472 | tf_op jit(solution)/shard_map/reduce_scatter | solution.py:308
  611.4 40.6 %reduce-scatter.12.cloned.1.call-done = bf16[96,768]{1,0:T(8,128)(2,1)} async-done(((bf16[768,768]{1,0:T(8,128)(2,1)}), bf16[96,768]{1,0:T(8,128)(2,1)}) %reduce-scatter.12.cloned.1.call-update) | async-done | bytes 147472 | tf_op jit(solution)/shard_map/reduce_scatter | solution.py:302
  652.0 40.8 %reduce-scatter.14.cloned.1.call-done = bf16[96,768]{1,0:T(8,128)(2,1)} async-done(((bf16[768,768]{1,0:T(8,128)(2,1)}), bf16[96,768]{1,0:T(8,128)(2,1)}) %reduce-scatter.14.cloned.1.call-update) | async-done | bytes 147472 | tf_op jit(solution)/shard_map/reduce_scatter | solution.py:305
  692.8 8.7 fusion.15
  701.5 8.3 pad_maximum_fusion
  709.9 23.9 %copy.108 = bf16[2,768,3072]{1,0,2:T(2,128)(2,1)} copy(bf16[2,768,3072]{2,1,0:T(8,128)(2,1)} %pad_maximum_fusion) | data formatting | bytes 18874368
  733.8 9.0 copy.116
  744.3 9.0 fusion.18
  753.3 8.0 fusion.17
  761.2 8.3 pad_maximum_fusion.1
  769.6 8.7 copy.113
  778.3 11.6 %pad.10.clone = bf16[12,512,1023]{2,1,0:T(8,128)(2,1)} pad(bf16[12,512,512]{2,1,0:T(8,128)(2,1)} %copy.113, bf16[]{:T(256)} %constant.8.clone.1), padding=0_0x0_0x0_511 | pad | bytes 18862082 | tf_op jit(solution)/shard_map/jit(_pad)/pad | solution.py:67
  789.9 35.7 %reshape.299 = bf16[12,523776]{1,0:T(8,128)(2,1)} reshape(bf16[12,512,1023]{2,1,0:T(8,128)(2,1)} %pad.10.clone) | data formatting | bytes 25141248 | tf_op jit(solution)/shard_map/reshape | solution.py:68
  825.6 8.6 pad_convert_fusion
  834.2 36.3 %copy.115 = f32[2,8,512,1024]{3,2,1,0:T(8,128)} copy(f32[2,8,512,1024]{3,1,2,0:T(8,128)S(1)} %bitcast.162) | data formatting | bytes 67108864
  870.5 9.8 %slice_reduce_fusion = f32[12,1024]{1,0:T(8,128)S(1)} fusion(f32[16,512,1024]{2,1,0:T(8,128)} %bitcast.163), kind=kLoop, calls=%fused_computation | loop fusion | flops 6279168 | bytes 25214976 | tf_op jit(solution)/shard_map/reduce_sum | solution.py:69
  888.8 23.7 %all-reduce.7 = (bf16[768]{0:T(1024)(128)(2,1)S(1)}, bf16[768]{0:T(1024)(128)(2,1)S(1)}, bf16[32,12]{1,0:T(8,128)(2,1)S(1)}) all-reduce(bf16[768]{0:T(1024)(128)(2,1)S(1)} %get-tuple-element.16, bf16[768]{0:T(1024)(128)(2,1)S(1)} %get-tuple-element.12, ...), channel_id=7, replica_groups=mesh['dp'=8,'expert'=4] {'dp'}, use_global_device_ids=true, to_apply=%region_27.28.clone | all-reduce | flops 1920 | bytes 7680
  916.2 11.7 %all-reduce.9 = (bf16[96,8]{0,1:T(8,128)(2,1)S(1)}, bf16[96]{0:T(256)(128)(2,1)S(1)}, bf16[96]{0:T(256)(128)(2,1)S(1)}, bf16[4,12]{1,0:T(4,128)(2,1)S(1)}) all-reduce(bf16[96,8]{0,1:T(8,128)(2,1)S(1)} %copy.107, bf16[96]{0:T(256)(128)(2,1)S(1)} %dynamic-slice.3, ...), channel_id=1, replica_groups=mesh['dp'=8,'expert'=4] {'expert'}, use_global_device_ids=true, to_apply=%region_25.26 | all-reduce | flops 1008 | bytes 4032 | tf_op jit(solution)/shard_map/psum | solution.py:332
  (271 shorter events, 134.3 us)
Async XLA Ops:
  7.2 179.6 %all-gather.11.cloned.1.call-start = ((), (), s32[]{:S(2)}) async-start(), calls=%async_computation.12 | async-start | bytes 1327104 | tf_op jit(solution)/shard_map/all_gather | solution.py:136
  7.9 181.3 %all-gather.13.cloned.1.call-start = ((), (), s32[]{:S(2)}) async-start(), calls=%async_computation.13 | async-start | bytes 1327104 | tf_op jit(solution)/shard_map/all_gather | solution.py:137
  8.7 183.2 %all-gather.9.cloned.1.call-start = ((), (), s32[]{:S(2)}) async-start(), calls=%async_computation.11 | async-start | bytes 1327104 | tf_op jit(solution)/shard_map/all_gather | solution.py:135
  9.4 199.6 %all-gather.15.cloned.1.call-start = ((), (), s32[]{:S(2)}) async-start(), calls=%async_computation.14 | async-start | bytes 1327104 | tf_op jit(solution)/shard_map/all_gather | solution.py:138
  10.0 331.3 %all-gather.17.cloned.1.call-start = ((), (), s32[]{:S(2)}) async-start(), calls=%async_computation.15 | async-start | bytes 10616832 | tf_op jit(solution)/shard_map/all_gather | solution.py:145
  38.9 153.0 %copy-start.37 = (f32[768]{0:T(1024)}, f32[768]{0:T(1024)S(1)}, u32[]{:S(2)}) copy-start(f32[768]{0:T(1024)S(1)} %convert_element_type.228) | copy-start | bytes 9220
  38.9 172.7 %copy-start.33 = (f32[768]{0:T(1024)}, f32[768]{0:T(1024)S(1)}, u32[]{:S(2)}) copy-start(f32[768]{0:T(1024)S(1)} %convert_element_type.240) | copy-start | bytes 9220
  48.3 164.6 %copy-start.31 = (bf16[768,8]{0,1:T(8,128)(2,1)}, bf16[768,8]{0,1:T(8,128)(2,1)S(1)}, u32[]{:S(2)}) copy-start(bf16[768,8]{0,1:T(8,128)(2,1)S(1)} %reshape.313) | copy-start | bytes 36868
  177.2 9.3 copy-start.10
  186.7 46.4 %copy-start.49 = (s32[1024]{0:T(1024)}, s32[1024]{0:T(1024)S(1)}, u32[]{:S(2)}) copy-start(s32[1024]{0:T(1024)S(1)} %convert_add_fusion.1) | copy-start | bytes 12292
  189.2 7.4 copy-start.6
  191.9 12.2 %copy-start.8 = (bf16[512,768]{0,1:T(8,128)(2,1)}, bf16[512,768]{0,1:T(8,128)(2,1)S(1)}, u32[]{:S(2)}) copy-start(bf16[512,768]{0,1:T(8,128)(2,1)S(1)} %copy.85) | copy-start | bytes 2359300
  211.5 9.6 %copy-start.53 = (f32[512]{0:T(512)}, f32[512]{0:T(512)S(1)}, u32[]{:S(2)}) copy-start(f32[512]{0:T(512)S(1)} %get-tuple-element.45) | copy-start | bytes 6148
  212.9 13.7 %copy-start.4 = (bf16[512,768]{1,0:T(8,128)(2,1)}, bf16[512,768]{1,0:T(8,128)(2,1)S(1)}, u32[]{:S(2)}) copy-start(bf16[512,768]{1,0:T(8,128)(2,1)S(1)} %multiply_convert_fusion.7) | copy-start | bytes 2359300
  221.1 59.6 %all-to-all-start.2 = ((bf16[4,2,192,768]{3,2,1,0:T(8,128)(2,1)}), bf16[4,2,192,768]{3,2,1,0:T(8,128)(2,1)S(1)}, u32[]{:S(2)}, u32[]{:S(2)}) async-start(bf16[4,2,192,768]{3,2,1,0:T(8,128)(2,1)} %bitcast.183), calls=%async_computation.2 | async-start | bytes 4718592 | tf_op jit(solution)/shard_map/all_to_all | solution.py:241
  226.0 168.2 %all-gather.19.cloned.1.call-start = ((), (), s32[]{:S(2)}) async-start(), calls=%async_computation.16 | async-start | bytes 10616832 | tf_op jit(solution)/shard_map/all_gather | solution.py:146
  280.7 58.7 %all-to-all-start = ((bf16[4,2,192,768]{3,2,1,0:T(8,128)(2,1)}), bf16[4,2,192,768]{3,2,1,0:T(8,128)(2,1)}, u32[]{:S(2)}, u32[]{:S(2)}) async-start(bf16[4,2,192,768]{3,2,1,0:T(8,128)(2,1)} %bitcast.184), calls=%async_computation | async-start | bytes 4718592 | tf_op jit(solution)/shard_map/all_to_all | solution.py:198
  341.2 27.3 %copy-start.26 = (bf16[4,1,192,768]{3,2,1,0:T(8,128)(2,1)}, bf16[4,1,192,768]{3,2,1,0:T(8,128)(2,1)S(1)}, u32[]{:S(2)}) copy-start(bf16[4,1,192,768]{3,2,1,0:T(8,128)(2,1)S(1)} %get-tuple-element.38) | copy-start | bytes 3538948
  341.2 27.3 %copy-start.25 = (bf16[4,1,192,768]{3,2,1,0:T(8,128)(2,1)}, bf16[4,1,192,768]{3,2,1,0:T(8,128)(2,1)S(1)}, u32[]{:S(2)}) copy-start(bf16[4,1,192,768]{3,2,1,0:T(8,128)(2,1)S(1)} %get-tuple-element.37) | copy-start | bytes 3538948
  341.3 27.2 %copy-start.55 = (bf16[2,768,3072]{2,1,0:T(8,128)(2,1)S(1)}, bf16[2,768,3072]{2,1,0:T(8,128)(2,1)}, u32[]{:S(2)}) copy-start(bf16[2,768,3072]{2,1,0:T(8,128)(2,1)} %all-gather.17.cloned.1.call-done) | copy-start | bytes 28311556
  394.2 7.7 copy-start.56
  394.3 7.8 copy-start.61
  407.5 58.1 %all-to-all-start.1 = ((bf16[4,2,192,768]{3,2,1,0:T(8,128)(2,1)}), bf16[4,2,192,768]{3,2,1,0:T(8,128)(2,1)}, u32[]{:S(2)}, u32[]{:S(2)}) async-start(bf16[4,2,192,768]{3,2,1,0:T(8,128)(2,1)} %pad_maximum_fusion.2), calls=%async_computation.1 | async-start | bytes 4718592 | tf_op jit(solution)/shard_map/all_to_all | solution.py:217
  423.0 8.0 copy-start.60
  423.1 8.0 copy-start.22
  423.1 19.2 %slice-start = ((s8[9437184]{0:T(1024)(128)(4,1)}), s8[4194304]{0:T(1024)(128)(4,1)S(1)}, s32[]{:S(2)}) async-start(s8[9437184]{0:T(1024)(128)(4,1)} %bitcast.202), calls=%async_computation.25 | async-start | bytes 8388608
  431.0 11.3 %slice-start.1 = ((s8[9437184]{0:T(1024)(128)(4,1)}), s8[4194304]{0:T(1024)(128)(4,1)S(1)}, s32[]{:S(2)}) async-start(s8[9437184]{0:T(1024)(128)(4,1)} %bitcast.202), calls=%async_computation.26 | async-start | bytes 8388608
  431.1 11.3 %slice-start.2 = ((s8[9437184]{0:T(1024)(128)(4,1)}), s8[1048576]{0:T(1024)(128)(4,1)S(1)}, s32[]{:S(2)}) async-start(s8[9437184]{0:T(1024)(128)(4,1)} %bitcast.202), calls=%async_computation.27 | async-start | bytes 2097152
  446.2 24.1 %copy-start.13 = (bf16[512,768]{1,0:T(8,128)(2,1)S(1)}, bf16[512,768]{1,0:T(8,128)(2,1)}, u32[]{:S(2)}) copy-start(bf16[512,768]{1,0:T(8,128)(2,1)} %param.27) | copy-start | bytes 2359300
  447.9 23.8 %copy-start.50 = (s32[1024]{0:T(1024)S(1)}, s32[1024]{0:T(1024)}, u32[]{:S(2)}) copy-start(s32[1024]{0:T(1024)} %copy-done.49) | copy-start | bytes 12292
  465.6 57.9 %all-to-all-start.3 = ((bf16[4,2,192,768]{3,2,1,0:T(8,128)(2,1)}), bf16[4,2,192,768]{3,2,1,0:T(8,128)(2,1)}, u32[]{:S(2)}, u32[]{:S(2)}) async-start(bf16[4,2,192,768]{3,2,1,0:T(8,128)(2,1)} %pad_maximum_fusion.3), calls=%async_computation.3 | async-start | bytes 4718592 | tf_op jit(solution)/shard_map/all_to_all | solution.py:264
  470.1 117.9 %reduce-scatter.18.cloned.1.call-start = ((), (), s32[]{:S(2)}) async-start(), calls=%async_computation.20 | async-start | bytes 1327104 | tf_op jit(solution)/shard_map/reduce_scatter | solution.py:311
  535.9 75.5 %reduce-scatter.16.cloned.1.call-start = ((), (), s32[]{:S(2)}) async-start(), calls=%async_computation.19 | async-start | bytes 1327104 | tf_op jit(solution)/shard_map/reduce_scatter | solution.py:308
  536.4 7.8 copy-start.11
  536.4 7.8 copy-start.38
  536.4 7.8 copy-start.46
  536.4 9.7 %copy-start.9 = (bf16[512,768]{0,1:T(8,128)(2,1)S(1)}, bf16[512,768]{0,1:T(8,128)(2,1)}, u32[]{:S(2)}) copy-start(bf16[512,768]{0,1:T(8,128)(2,1)} %copy-done.8) | copy-start | bytes 2359300
  555.1 96.8 %reduce-scatter.12.cloned.1.call-start = ((), (), s32[]{:S(2)}) async-start(), calls=%async_computation.17 | async-start | bytes 1327104 | tf_op jit(solution)/shard_map/reduce_scatter | solution.py:302
  555.2 9.9 %copy-start.7 = (bf16[512,768]{0,1:T(8,128)(2,1)S(1)}, bf16[512,768]{0,1:T(8,128)(2,1)}, u32[]{:S(2)}) copy-start(bf16[512,768]{0,1:T(8,128)(2,1)} %copy-done.6) | copy-start | bytes 2359300
  569.7 8.1 copy-start.5
  569.8 123.0 %reduce-scatter.14.cloned.1.call-start = ((), (), s32[]{:S(2)}) async-start(), calls=%async_computation.18 | async-start | bytes 1327104 | tf_op jit(solution)/shard_map/reduce_scatter | solution.py:305
  577.8 337.6 %reduce-scatter.22.cloned.1.call-start = ((), (), s32[]{:S(2)}) async-start(), calls=%async_computation.22 | async-start | bytes 221184
  578.9 351.2 %all-reduce.13.cloned.1.call-start = ((), (), s32[]{:S(2)}) async-start(), calls=%async_computation.24 | async-start | bytes 1179648 | tf_op jit(solution)/shard_map/psum | solution.py:328
  692.8 243.9 %reduce-scatter.24.cloned.1.call-start = ((), (), s32[]{:S(2)}) async-start(), calls=%async_computation.23 | async-start | bytes 10616832
  742.8 200.4 %reduce-scatter.20.cloned.1.call-start = ((), (), s32[]{:S(2)}) async-start(), calls=%async_computation.21 | async-start | bytes 10616832 | tf_op jit(solution)/shard_map/reduce_scatter | solution.py:341
  744.3 9.0 copy-start.23
  870.5 10.2 %copy-start.57 = (s32[512]{0:T(512)S(1)}, s32[512]{0:T(512)}, u32[]{:S(2)}) copy-start(s32[512]{0:T(512)} %param.26) | copy-start | bytes 6148
  884.1 28.5 %copy-start.48 = (f32[512]{0:T(512)S(1)}, f32[512]{0:T(512)}, u32[]{:S(2)}) copy-start(f32[512]{0:T(512)} %copy-done.47) | copy-start | bytes 6148
  (35 other events, 135.8 us)
Sparse Core Ops, SparseCore 0:
  9.9 26.8 all-gather.10
  38.7 24.0 all-gather.12
  64.7 24.0 all-gather.8
  90.5 24.0 all-gather.14
  116.3 60.5 all-gather.16
  228.4 59.8 all-gather.18
  536.0 34.9 reduce-scatter.17
  574.6 36.7 reduce-scatter.15
  615.2 36.7 reduce-scatter.11
  655.9 36.7 reduce-scatter.13
  696.4 33.4 reduce-scatter.21
  732.5 39.8 all-reduce.12
  776.3 75.9 reduce-scatter.23
  856.0 76.9 reduce-scatter.19
where the time goes:
time: 963 us; the launch traced here: 953 us
  local copies, waits for them, and re-layouts  299 us (31%)
  waiting for transfers between devices  260 us (27%)
  matrix products  217 us (23%)
  other arithmetic  70.3 us (7%)
  blocking collectives  67.9 us (7%)
  starting transfers between devices  20.4 us (2%)
  between operations  17.2 us (2%)
    unnamed x155, local copies, waits for them, and re-layouts  166 us
    dot_general x13, matrix products, product(): return jnp.dot(left, right, preferred_element_type=jnp.float32)  88.1 us
    dot_general x11, matrix products, product_tn(): lax.dot_general(left, right, (((0,), (0,)), ((), ())), preferred_element_...  55 us
    all_to_all x1, waiting for transfers between devices, body(): lax.all_to_all(filled.reshape(owners, local_count, capacity, width), 'exp...  52.3 us
    reshape x1, local copies, waits for them, and re-layouts, bias_block(): tiled.reshape(heads, block, period - 1)[:, :, :seq_len].astype(jnp.float32)  44.3 us
    dot_general x9, matrix products, product_nt(): lax.dot_general(left, right, (((1,), (1,)), ((), ())), preferred_element_...  44.3 us
    all_to_all x1, waiting for transfers between devices, body(): lax.all_to_all(grad_returned.reshape(owners, local_count, capacity, width...  42.1 us
    reduce_scatter x1, waiting for transfers between devices, body(): lax.psum_scatter(grad_key_w.astype(jnp.bfloat16), 'dp', scatter_dimension...  40.8 us
  transfers between devices with their start and end apart: 18, of which 7 were waited for; matrix products, arithmetic and copies ran while one was open for 58% of the time, Pallas kernels for 0%

commit v1 on v0

v1 whole, which is shorter than its diff:
```python
import functools

import jax
import jax.numpy as jnp
from jax import lax
from jax.experimental import pallas as pl
from jax.experimental.pallas import tpu as pltpu
from jax.sharding import PartitionSpec as P

HEADS = 12
HEAD_DIM = 64
EPSILON = 1e-06
NEGATIVE = -1e30
SCALE = HEAD_DIM ** (-0.5)
LANES = 128
TABLE_AT = 32
QBLOCK = 256
F32 = jnp.float32
BF16 = jnp.bfloat16
I32 = jnp.int32
VMEM_LIMIT = 60 * 1024 * 1024


def nn(left, right):
    return lax.dot_general(left, right, (((1,), (0,)), ((), ())), preferred_element_type=F32)


def nt(left, right):
    return lax.dot_general(left, right, (((1,), (1,)), ((), ())), preferred_element_type=F32)


def tn(left, right):
    return lax.dot_general(left, right, (((0,), (0,)), ((), ())), preferred_element_type=F32)


def iota(shape, axis):
    return lax.broadcasted_iota(I32, shape, axis)


def hot(mask):
    return jnp.where(mask, 1.0, 0.0).astype(BF16)


def vmem_call(body, name, out_shape, scratch=(), flops=0, moved=0, specs=None):
    def call(*args):
        in_specs = specs or [pl.BlockSpec(memory_space=pltpu.VMEM)] * len(args)
        return pl.pallas_call(
            body,
            name=name,
            out_shape=out_shape,
            in_specs=in_specs,
            out_specs=jax.tree.map(lambda _: pl.BlockSpec(memory_space=pltpu.VMEM), out_shape),
            scratch_shapes=scratch,
            compiler_params=pltpu.CompilerParams(vmem_limit_bytes=VMEM_LIMIT),
            cost_estimate=pl.CostEstimate(flops=flops, bytes_accessed=moved, transcendentals=0),
        )(*args)

    return call


def places(r, slot, here, local, cap):
    owner = lax.div(r, local)
    return (owner ^ here) * (local * cap) + lax.rem(r, local) * cap + slot.astype(I32)


def places_by_lane(routes_t, here, experts, local, cap):
    n = routes_t.shape[1]
    r0, r1 = routes_t[0:1, :], routes_t[1:2, :]
    tall = iota((-(-experts // 16) * 16, n), 0)
    oh0, oh1 = tall == r0, tall == r1
    earlier = hot(iota((n, n), 0) < iota((n, n), 1))
    count = nn(hot(oh0 | oh1), earlier)
    s0 = jnp.sum(jnp.where(oh0, count, 0.0), axis=0, keepdims=True)
    s1 = jnp.sum(jnp.where(oh1, count, 0.0), axis=0, keepdims=True)
    return places(r0, s0, here, local, cap), places(r1, s1, here, local, cap)


def places_by_row(routes, here, local, cap):
    n = routes.shape[0]
    r0, r1 = routes[:, 0:1], routes[:, 1:2]
    wide = iota((n, LANES), 1)
    oh0, oh1 = wide == r0, wide == r1
    earlier = hot(iota((n, n), 1) < iota((n, n), 0))
    count = nn(earlier, hot(oh0 | oh1))
    s0 = jnp.sum(jnp.where(oh0, count, 0.0), axis=1, keepdims=True)
    s1 = jnp.sum(jnp.where(oh1, count, 0.0), axis=1, keepdims=True)
    return places(r0, s0, here, local, cap), places(r1, s1, here, local, cap), oh0, oh1


def put_rows(values, d0, d1, start, count):
    at = iota((count, values.shape[0]), 0) + start
    return nn(hot((at == d0) | (at == d1)), values).astype(BF16)


def scatter_kernel(experts, local, cap, here_ref, routes_t_ref, values_ref, *out_refs):
    d0, d1 = places_by_lane(routes_t_ref[...], here_ref[0], experts, local, cap)
    values = values_ref[...]
    for at, out_ref in enumerate(out_refs):
        out_ref[...] = put_rows(values, d0, d1, at * cap, cap)


def table_rows(misc, buckets, shards):
    depth = misc.shape[0]
    per, rows = buckets // shards, depth // shards
    b = iota((buckets, depth), 0)
    select = hot(iota((buckets, depth), 1) == lax.div(b, per) * rows + lax.rem(b, per))
    return nn(select, misc)


def toeplitz(line, twice_ref):
    n = line.shape[1]
    rolled = pltpu.roll(jnp.broadcast_to(line, (LANES, n)), 0, 1, stride=1, stride_axis=0)
    twice_ref[:, :n] = rolled
    twice_ref[:, n:] = rolled


def bias_columns(twice_ref, n, block, rows):
    parts = []
    for jb in range(rows // LANES):
        start = (block * QBLOCK - jb * LANES) % n
        parts.append(twice_ref[:, start : start + QBLOCK])
    return jnp.concatenate(parts, axis=0)


def causal(scores, block):
    last = scores.shape[0] - QBLOCK
    keep = iota((QBLOCK, QBLOCK), 0) <= iota((QBLOCK, QBLOCK), 1)
    tail = jnp.where(keep, scores[last:], NEGATIVE)
    return tail if last == 0 else jnp.concatenate([scores[:last], tail], axis=0)


def forward_kernel(
    experts,
    local,
    cap,
    buckets,
    shards,
    here_ref,
    tok_ref,
    w_ref,
    routes_ref,
    routes_t_ref,
    bucket_ref,
    q_ref,
    k_ref,
    v_ref,
    normed_ref,
    merged_t_ref,
    middle_ref,
    second_ref,
    gates_ref,
    line_ref,
    *rest,
):
    groups = experts // local
    x_refs, slot_refs = rest[:experts], rest[experts : experts + groups]
    v_t_ref, out_t_ref, twice_ref = rest[experts + groups :]
    n, width = tok_ref.shape
    misc = w_ref[:, 4 * width :]
    misc_t = jnp.transpose(misc.astype(F32))
    gain_one, gain_two = misc_t[experts : experts + 1], misc_t[experts + 1 : experts + 2]
    x = tok_ref[...].astype(F32)
    normed = x * lax.rsqrt(jnp.mean(x * x, axis=-1, keepdims=True) + EPSILON) * gain_one
    normed_ref[...] = normed.astype(BF16)
    normed = normed_ref[...]
    q_ref[...] = (nn(normed, w_ref[:, :width]).astype(BF16).astype(F32) * SCALE).astype(BF16)
    k_ref[...] = nn(normed, w_ref[:, width : 2 * width]).astype(BF16)
    value = nn(normed, w_ref[:, 2 * width : 3 * width]).astype(BF16)
    v_ref[...] = value
    v_t_ref[...] = jnp.transpose(value)
    table = table_rows(misc, buckets, shards).astype(BF16)
    by_bucket = hot(iota((buckets, n), 0) == bucket_ref[...])
    line_ref[...] = tn(table, by_bucket)[TABLE_AT : TABLE_AT + 16]
    half = iota((1, LANES), 1) < HEAD_DIM

    def pair(hp, carry):
        lanes = pl.ds(pl.multiple_of(hp * LANES, LANES), LANES)
        kp, qp = k_ref[:, lanes], q_ref[:, lanes]
        for side in range(2):
            toeplitz(line_ref[pl.ds(hp * 2 + side, 1), :], twice_ref)
            keys = kp * hot(half if side == 0 else ~half)
            at = pl.ds(pl.multiple_of(hp * LANES + side * HEAD_DIM, HEAD_DIM), HEAD_DIM)
            for block in range(n // QBLOCK):
                rows = (block + 1) * QBLOCK
                cols = slice(block * QBLOCK, rows)
                scores = nt(keys[:rows], qp[cols]) + bias_columns(twice_ref, n, block, rows)
                scores = causal(scores, block)
                top = jnp.max(scores, axis=0, keepdims=True)
                e = jnp.exp(scores - top)
                probs = (e * (1.0 / jnp.sum(e, axis=0, keepdims=True))).astype(BF16)
                out_t_ref[at, cols] = nn(v_t_ref[at, :rows], probs).astype(BF16)
        return carry

    lax.fori_loop(0, HEADS // 2, pair, 0)
    merged_t_ref[...] = out_t_ref[...]
    middle = x + tn(merged_t_ref[...], w_ref[:, 3 * width : 4 * width])
    middle_ref[...] = middle
    second = middle * lax.rsqrt(jnp.mean(middle * middle, axis=-1, keepdims=True) + EPSILON)
    second_ref[...] = (second * gain_two).astype(BF16)
    second = second_ref[...]
    here = here_ref[0]
    c0, c1, oh0, oh1 = places_by_row(routes_ref[...], here, local, cap)
    logits = nn(second, misc)
    p0 = jnp.sum(jnp.where(oh0, logits, 0.0), axis=1, keepdims=True)
    p1 = jnp.sum(jnp.where(oh1, logits, 0.0), axis=1, keepdims=True)
    top = jnp.maximum(p0, p1)
    e0, e1 = jnp.exp(p0 - top), jnp.exp(p1 - top)
    g0, g1 = e0 / (e0 + e1), e1 / (e0 + e1)
    wide = iota((n, LANES), 1)
    gates_ref[...] = jnp.where(wide == 0, g0, jnp.where(wide == 1, g1, 0.0))
    d0, d1 = places_by_lane(routes_t_ref[...], here, experts, local, cap)
    for at, x_ref in enumerate(x_refs):
        x_ref[...] = put_rows(second, d0, d1, at * cap, cap)
    for at, slot_ref in enumerate(slot_refs):
        slot_ref[...] = jnp.zeros_like(slot_ref)
        for l in range(local):
            lane = iota((n, slot_ref.shape[1]), 1) + (at * local + l) * cap
            held = jnp.where(lane == c0, g0, jnp.where(lane == c1, g1, 0.0))
            slot_ref[l : l + 1, :] = jnp.sum(held, axis=0, keepdims=True)


def gelu_both(v):
    t = pl.reciprocal(1.0 + (0.3275911 * 0.7071067811865476) * jnp.abs(v))
    e = jnp.exp(-0.5 * (v * v))
    poly = 0.5 * 1.061405429
    for coefficient in (-1.453152027, 1.421413741, -0.284496736, 0.254829592):
        poly = poly * t + 0.5 * coefficient
    tail = poly * t * e
    phi = jnp.where(v < 0.0, tail, 1.0 - tail)
    return v * phi, phi + v * e * 0.3989422804014327


def expert_kernel(local_at, groups, cap, *refs):
    take = iter(refs)
    row_refs = [next(take) for _ in range(groups)]
    cot_refs = [next(take) for _ in range(groups)]
    slot_refs = [next(take) for _ in range(groups)]
    up_a, up_b, down_a, down_b = (next(take) for _ in range(4))
    reply_refs = [next(take) for _ in range(groups)]
    back_refs = [next(take) for _ in range(groups)]
    dot_refs = [next(take) for _ in range(groups)]
    ug_a, ug_b, dg_a, dg_b = (next(take) for _ in range(4))
    x_ref, xt_ref, cot_ref, gr_ref, reply_ref, back_ref = (next(take) for _ in range(6))
    up_buf, down_buf, ug_buf, dg_buf, act_ref, gh_ref = (next(take) for _ in range(6))
    in_sem, out_sem = next(take), next(take)
    rows, width = x_ref.shape
    slab = up_a.shape[2]
    block = up_buf.shape[2]
    per = block // slab
    half = up_a.shape[0] // per
    steps = 2 * half

    def fetches(up, down, at, slot):
        for i in range(per):
            cut = slice(i * slab, (i + 1) * slab)
            yield pltpu.make_async_copy(
                up.at[at * per + i], up_buf.at[slot, :, cut], in_sem.at[slot, i]
            )
            yield pltpu.make_async_copy(
                down.at[at + i * half], down_buf.at[slot, cut, :], in_sem.at[slot, per + i]
            )

    def stores(up, down, at, slot):
        for i in range(per):
            cut = slice(i * slab, (i + 1) * slab)
            yield pltpu.make_async_copy(
                ug_buf.at[slot, :, cut], up.at[at * per + i], out_sem.at[slot, i]
            )
            yield pltpu.make_async_copy(
                dg_buf.at[slot, cut, :], down.at[at + i * half], out_sem.at[slot, per + i]
            )

    def begin(kind, first, second, step, slot):
        @pl.when(step < half)
        def _():
            for copy in kind(*first, step, slot):
                copy.start()

        @pl.when(step >= half)
        def _():
            for copy in kind(*second, step - half, slot):
                copy.start()

    begin(fetches, (up_a, down_a), (up_b, down_b), 0, 0)
    for m in range(groups):
        cut = slice(m * cap, (m + 1) * cap)
        x_ref[cut, :] = row_refs[m][...]
        slots = jnp.broadcast_to(
            slot_refs[m][local_at : local_at + 1, :], (LANES, slot_refs[m].shape[1])
        )
        gate = jnp.transpose(slots)[:cap, 0:1]
        cot = cot_refs[m][...]
        cot_ref[cut, :] = cot
        gr_ref[cut, :] = (gate * cot.astype(F32)).astype(BF16)
    xt_ref[...] = jnp.transpose(x_ref[...])
    reply_ref[...] = jnp.zeros_like(reply_ref)
    back_ref[...] = jnp.zeros_like(back_ref)

    def step(at, carry):
        slot = lax.rem(at, 2)

        @pl.when(at + 1 < steps)
        def _():
            begin(fetches, (up_a, down_a), (up_b, down_b), at + 1, 1 - slot)

        for copy in fetches(up_a, down_a, 0, slot):
            copy.wait()

        @pl.when(at >= 2)
        def _():
            for copy in stores(ug_a, dg_a, 0, slot):
                copy.wait()

        chunk = 256
        for c in range(rows // chunk):
            cut = slice(c * chunk, (c + 1) * chunk)
            act, slope = gelu_both(nn(x_ref[cut, :], up_buf[slot]))
            act_ref[cut, :] = act.astype(BF16)
            grad = nt(gr_ref[cut, :], down_buf[slot])
            gh_ref[cut, :] = (grad * slope).astype(BF16)
            reply_ref[cut, :] += nn(act_ref[cut, :], down_buf[slot])
            back_ref[cut, :] += nt(gh_ref[cut, :], up_buf[slot])
        dg_buf[slot] = tn(act_ref[...], gr_ref[...]).astype(BF16)
        ug_buf[slot] = nn(xt_ref[...], gh_ref[...]).astype(BF16)
        begin(stores, (ug_a, dg_a), (ug_b, dg_b), at, slot)
        return carry

    lax.fori_loop(0, steps, step, 0)
    reply = reply_ref[...].astype(BF16)
    dots = jnp.sum(reply.astype(F32) * cot_ref[...].astype(F32), axis=1, keepdims=True)
    dots = jnp.transpose(jnp.broadcast_to(dots, (rows, LANES)))[0:8]
    for m in range(groups):
        cut = slice(m * cap, (m + 1) * cap)
        reply_refs[m][...] = reply[cut]
        back_refs[m][...] = back_ref[cut, :].astype(BF16)
        shifted = dots if m == 0 else pltpu.roll(dots, rows - m * cap, 1)
        dot_refs[m][...] = shifted[:, : dot_refs[m].shape[1]]
    for slot in range(2):
        for copy in stores(ug_a, dg_a, 0, slot):
            copy.wait()


def backward_kernel(
    experts,
    local,
    cap,
    buckets,
    shards,
    here_ref,
    tok_ref,
    w_ref,
    routes_ref,
    bucket_ref,
    cot_ref,
    q_ref,
    k_ref,
    v_ref,
    normed_ref,
    merged_t_ref,
    middle_ref,
    second_ref,
    gates_ref,
    line_ref,
    *rest,
):
    groups = experts // local
    take = iter(rest)
    back_refs = [next(take) for _ in range(experts)]
    dot_refs = [next(take) for _ in range(experts)]
    inputs_grad_ref, grads_ref = next(take), next(take)
    gm_ref, gmid_ref, k_t_ref, gq_t_ref, gk_ref, gv_ref, fold_ref, twice_ref = take
    n, width = tok_ref.shape
    misc = w_ref[:, 4 * width :]
    misc_t = jnp.transpose(misc.astype(F32))
    gain_one, gain_two = misc_t[experts : experts + 1], misc_t[experts + 1 : experts + 2]
    c0, c1, oh0, oh1 = places_by_row(routes_ref[...], here_ref[0], local, cap)
    grad_second = jnp.zeros((n, width), F32)
    gg0 = jnp.zeros((n, 1), F32)
    gg1 = jnp.zeros((n, 1), F32)
    for at in range(experts):
        lane = iota((n, cap), 1) + at * cap
        h0, h1 = lane == c0, lane == c1
        grad_second += nn(hot(h0 | h1), back_refs[at][...])
        dots = dot_refs[at][0:1, :cap]
        gg0 += jnp.sum(jnp.where(h0, dots, 0.0), axis=1, keepdims=True)
        gg1 += jnp.sum(jnp.where(h1, dots, 0.0), axis=1, keepdims=True)
    g0, g1 = gates_ref[:, 0:1], gates_ref[:, 1:2]
    inner = g0 * gg0 + g1 * gg1
    grad_logits = jnp.where(oh0, g0 * (gg0 - inner), jnp.where(oh1, g1 * (gg1 - inner), 0.0))
    grad_logits = grad_logits.astype(BF16)
    grad_second += nt(grad_logits, misc)
    router_grad = tn(second_ref[...], grad_logits)
    middle = middle_ref[...]
    r = lax.rsqrt(jnp.mean(middle * middle, axis=-1, keepdims=True) + EPSILON)
    mr = middle * r
    midnorm_grad = jnp.sum(grad_second * mr, axis=0, keepdims=True)
    u = gain_two * grad_second
    gmid = cot_ref[...].astype(F32) + r * (u - mr * jnp.mean(u * mr, axis=-1, keepdims=True))
    gmid_ref[...] = gmid
    branch = gmid.astype(BF16)
    grads_ref[:, 3 * width : 4 * width] = nn(merged_t_ref[...], branch).astype(BF16)
    gm_ref[...] = nt(branch, w_ref[:, 3 * width : 4 * width]).astype(BF16)
    k_t_ref[...] = jnp.transpose(k_ref[...])
    half = iota((1, LANES), 1) < HEAD_DIM

    def pair(hp, carry):
        lanes = pl.ds(pl.multiple_of(hp * LANES, LANES), LANES)
        kp, qp, vp, gp = k_ref[:, lanes], q_ref[:, lanes], v_ref[:, lanes], gm_ref[:, lanes]
        gk = [jnp.zeros((QBLOCK, LANES), F32) for _ in range(n // QBLOCK)]
        gv = [jnp.zeros((QBLOCK, LANES), F32) for _ in range(n // QBLOCK)]
        for side in range(2):
            toeplitz(line_ref[pl.ds(hp * 2 + side, 1), :], twice_ref)
            own = hot(half if side == 0 else ~half)
            keys, values, queries, outs = kp * own, vp * own, qp * own, gp * own
            at = pl.ds(pl.multiple_of(hp * LANES + side * HEAD_DIM, HEAD_DIM), HEAD_DIM)
            folded = jnp.zeros((LANES, n), F32)
            for block in range(n // QBLOCK):
                rows = (block + 1) * QBLOCK
                cols = slice(block * QBLOCK, rows)
                scores = nt(keys[:rows], qp[cols]) + bias_columns(twice_ref, n, block, rows)
                scores = causal(scores, block)
                top = jnp.max(scores, axis=0, keepdims=True)
                e = jnp.exp(scores - top)
                probs = e * (1.0 / jnp.sum(e, axis=0, keepdims=True))
                grad_probs = nt(values[:rows], gp[cols])
                total = jnp.sum(probs * grad_probs, axis=0, keepdims=True)
                gs = (probs * (grad_probs - total)).astype(BF16)
                low = probs.astype(BF16)
                gq_t_ref[at, cols] = (nn(k_t_ref[at, :rows], gs) * SCALE).astype(BF16)
                gk_part = nn(gs, queries[cols])
                gv_part = nn(low, outs[cols])
                for b in range(block + 1):
                    cut = slice(b * QBLOCK, (b + 1) * QBLOCK)
                    gk[b] += gk_part[cut]
                    gv[b] += gv_part[cut]
                wide = gs.astype(F32)
                for jb in range(rows // LANES):
                    piece = wide[jb * LANES : (jb + 1) * LANES]
                    parts = []
                    for lb in range(n // LANES):
                        src = (lb + jb) % (n // LANES) - block * (QBLOCK // LANES)
                        inside = 0 <= src < QBLOCK // LANES
                        parts.append(
                            piece[:, src * LANES : (src + 1) * LANES]
                            if inside
                            else jnp.zeros((LANES, LANES), F32)
                        )
                    folded += jnp.concatenate(parts, axis=1)
            size = LANES
            while size > 8:
                size //= 2
                folded = folded[:size] + pltpu.roll(folded[size : 2 * size], n - size, 1)
            fold_ref[hp * 2 + side] = folded
        for b in range(n // QBLOCK):
            cut = slice(b * QBLOCK, (b + 1) * QBLOCK)
            gk_ref[cut, lanes] = gk[b].astype(BF16)
            gv_ref[cut, lanes] = gv[b].astype(BF16)
        return carry

    lax.fori_loop(0, HEADS // 2, pair, 0)
    folded = fold_ref[...].reshape(HEADS * 8, n)
    row = iota((HEADS * 8, n), 0)
    for bit in (1, 2, 4):
        folded = jnp.where((row & bit) != 0, pltpu.roll(folded, n - bit, 1), folded)
    by_distance = jnp.sum(folded.reshape(HEADS, 8, n), axis=1)
    by_distance = jnp.concatenate([by_distance, jnp.zeros((16 - HEADS, n), F32)], axis=0)
    by_bucket = hot(iota((buckets, n), 0) == bucket_ref[...])
    table_grad = jnp.zeros((buckets, 16), F32)
    for _ in range(3):
        piece = by_distance.astype(BF16)
        table_grad += nt(by_bucket, piece)
        by_distance = by_distance - piece.astype(F32)
    spread = hot(iota((16, LANES), 1) == iota((16, LANES), 0) + TABLE_AT)
    table_grad = nn(table_grad.astype(BF16), spread).astype(BF16)
    rows, per = width // shards, buckets // shards
    b = iota((width, buckets), 1)
    select = hot(iota((width, buckets), 0) == lax.div(b, per) * rows + lax.rem(b, per))
    gq_t = gq_t_ref[...]
    gq = jnp.transpose(gq_t)
    gk, gv = gk_ref[...], gv_ref[...]
    normed_t = jnp.transpose(normed_ref[...])
    grads_ref[:, :width] = nt(normed_t, gq_t).astype(BF16)
    grads_ref[:, width : 2 * width] = nn(normed_t, gk).astype(BF16)
    grads_ref[:, 2 * width : 3 * width] = nn(normed_t, gv).astype(BF16)
    grad_normed = nt(gq, w_ref[:, :width])
    grad_normed += nt(gk, w_ref[:, width : 2 * width])
    grad_normed += nt(gv, w_ref[:, 2 * width : 3 * width])
    x = tok_ref[...].astype(F32)
    q = lax.rsqrt(jnp.mean(x * x, axis=-1, keepdims=True) + EPSILON)
    xq = x * q
    prenorm_grad = jnp.sum(grad_normed * xq, axis=0, keepdims=True)
    w = gain_one * grad_normed
    back = q * (w - xq * jnp.mean(w * xq, axis=-1, keepdims=True))
    inputs_grad_ref[...] = (gmid_ref[...] + back).astype(BF16)
    tall = iota((LANES, width), 0)
    gains = jnp.where(tall == experts, prenorm_grad, jnp.where(tall == experts + 1, midnorm_grad, 0.0))
    small = router_grad + jnp.transpose(gains) + nn(select, table_grad)
    grads_ref[:, 4 * width :] = small.astype(BF16)


def combine_kernel(local, cap, here_ref, routes_ref, gates_ref, middle_ref, *rest):
    *reply_refs, out_ref = rest
    n, width = middle_ref.shape
    c0, c1, _, _ = places_by_row(routes_ref[...], here_ref[0], local, cap)
    picked0 = jnp.zeros((n, width), F32)
    picked1 = jnp.zeros((n, width), F32)
    for at, reply_ref in enumerate(reply_refs):
        lane = iota((n, cap), 1) + at * cap
        picked0 += nn(hot(lane == c0), reply_ref[...])
        picked1 += nn(hot(lane == c1), reply_ref[...])
    out = middle_ref[...] + gates_ref[:, 0:1] * picked0 + gates_ref[:, 1:2] * picked1
    out_ref[...] = out.astype(BF16)


def swap(value, axis, bit):
    return lax.ppermute(value, axis, [(i, i ^ bit) for i in range(lax.axis_size(axis))])


def swap_all(values):
    return [v if m == 0 else swap(v, "expert", m) for m, v in enumerate(values)]


def gather_slabs(slab, bits):
    held = slab[None]
    for bit in bits[:-1]:
        held = jnp.concatenate([held, swap(held, "dp", bit)], axis=0)
    return held, swap(held, "dp", bits[-1])


def reduce_slabs(kept, sent, bits):
    def add(a, b):
        return a.astype(F32) + b.astype(F32)

    total = add(kept, swap(sent, "dp", bits[-1]))
    for bit in bits[-2::-1]:
        low = total.astype(BF16)
        half = low.shape[0] // 2
        total = add(low[:half], swap(low[half:], "dp", bit))
    return total[0]


def body(
    tokens,
    query_weight,
    key_weight,
    value_weight,
    project_weight,
    router_weight,
    prenorm_gain,
    midnorm_gain,
    bias_table,
    up_weight,
    down_weight,
    routes,
    bucket_index,
    cotangent,
):
    n, width = tokens.shape
    experts = router_weight.shape[1]
    shards, groups = lax.axis_size("dp"), lax.axis_size("expert")
    local, _, slab = up_weight.shape
    cap = 3 * n // experts
    buckets = bias_table.shape[0] * shards
    own_rows = query_weight.shape[0]
    hidden = slab * shards
    direct = slab % LANES == 0 and shards == 8
    here = lax.axis_index("expert").astype(I32).reshape(1)
    smem = pl.BlockSpec(memory_space=pltpu.SMEM)
    vmem = pl.BlockSpec(memory_space=pltpu.VMEM)
    hbm = pl.BlockSpec(memory_space=pl.ANY)
    routes_t = routes.T
    bucket_row = bucket_index[None, :]

    def shape(s, dtype=BF16):
        return jax.ShapeDtypeStruct(s, dtype)

    small = jnp.concatenate(
        [
            router_weight,
            prenorm_gain[:, None],
            midnorm_gain[:, None],
            jnp.zeros((own_rows, TABLE_AT - experts - 2), BF16),
            jnp.pad(bias_table, ((0, own_rows - bias_table.shape[0]), (0, 0))),
            jnp.zeros((own_rows, LANES - TABLE_AT - HEADS), BF16),
        ],
        axis=1,
    )
    packed = jnp.concatenate(
        [query_weight, key_weight, value_weight, project_weight, small], axis=1
    )
    full = lax.all_gather(packed, "dp", axis=0, tiled=True)

    cot_out = vmem_call(
        functools.partial(scatter_kernel, experts, local, cap),
        "send_cotangent",
        [shape((cap, width))] * experts,
        specs=[smem, vmem, vmem],
        flops=2 * n * experts * cap * width,
        moved=4 * experts * cap * width,
    )(here, routes_t, cotangent)
    cot_in = [swap_all(cot_out[l::local]) for l in range(local)]

    if direct:
        ups = [gather_slabs(up_weight[l], (2, 4, 1)) for l in range(local)]
        downs = [gather_slabs(down_weight[l], (4, 2, 1)) for l in range(local)]
    else:
        up_all = lax.all_gather(up_weight, "dp", axis=2, tiled=True)
        down_all = lax.all_gather(down_weight, "dp", axis=1, tiled=True)
        ups, downs = [], []
        for l in range(local):
            u = up_all[l].reshape(width, hidden // width, width).transpose(1, 0, 2)
            d = down_all[l].reshape(hidden // width, width, width)
            cut = hidden // width // 2
            ups.append((u[:cut], u[cut:]))
            downs.append((d[:cut], d[cut:]))

    forward = vmem_call(
        functools.partial(forward_kernel, experts, local, cap, buckets, shards),
        "attention_forward",
        [shape((n, width))] * 4
        + [
            shape((width, n)),
            shape((n, width), F32),
            shape((n, width)),
            shape((n, LANES), F32),
            shape((16, n), F32),
        ]
        + [shape((cap, width))] * experts
        + [shape((8, 256), F32)] * groups,
        scratch=[
            pltpu.VMEM((width, n), BF16),
            pltpu.VMEM((width, n), BF16),
            pltpu.VMEM((LANES, 2 * n), F32),
        ],
        specs=[smem] + [vmem] * 5,
        flops=20 * 10**9,
        moved=20 * 10**6,
    )(here, tokens, full, routes, routes_t, bucket_row)
    q, k, v, normed, merged_t, middle, second, gates, line = forward[:9]
    x_out, slots_out = forward[9 : 9 + experts], forward[9 + experts :]
    slots_in = swap_all(slots_out)
    x_in = [swap_all(x_out[l::local]) for l in range(local)]

    rows = groups * cap
    replies, backs, dots, up_grads, down_grads = [], [], [], [], []
    for l in range(local):
        up, down = ups[l], downs[l]
        count, slab_width = up[0].shape[0], up[0].shape[2]
        per = width // slab_width
        outs = pl.pallas_call(
            functools.partial(expert_kernel, l, groups, cap),
            name="expert",
            out_shape=[shape((cap, width))] * (2 * groups)
            + [shape((8, 256), F32)] * groups
            + [shape((count, width, slab_width))] * 2
            + [shape((count, slab_width, width))] * 2,
            in_specs=[vmem] * (3 * groups) + [hbm] * 4,
            out_specs=[vmem] * (3 * groups) + [hbm] * 4,
            scratch_shapes=[
                pltpu.VMEM((rows, width), BF16),
                pltpu.VMEM((width, rows), BF16),
                pltpu.VMEM((rows, width), BF16),
                pltpu.VMEM((rows, width), BF16),
                pltpu.VMEM((rows, width), F32),
                pltpu.VMEM((rows, width), F32),
                pltpu.VMEM((2, width, width), BF16),
                pltpu.VMEM((2, width, width), BF16),
                pltpu.VMEM((2, width, width), BF16),
                pltpu.VMEM((2, width, width), BF16),
                pltpu.VMEM((rows, width), BF16),
                pltpu.VMEM((rows, width), BF16),
                pltpu.SemaphoreType.DMA((2, 2 * per)),
                pltpu.SemaphoreType.DMA((2, 2 * per)),
            ],
            compiler_params=pltpu.CompilerParams(vmem_limit_bytes=VMEM_LIMIT),
            cost_estimate=pl.CostEstimate(
                flops=12 * rows * width * hidden, bytes_accessed=40 * 10**6, transcendentals=0
            ),
        )(*x_in[l], *cot_in[l], *slots_in, *up, *down)
        replies.append(outs[:groups])
        backs.append(swap_all(outs[groups : 2 * groups]))
        dots.append(swap_all(outs[2 * groups : 3 * groups]))
        ug, dg = outs[3 * groups : 3 * groups + 2], outs[3 * groups + 2 :]
        if direct:
            up_grads.append(reduce_slabs(*ug, (2, 4, 1)))
            down_grads.append(reduce_slabs(*dg, (4, 2, 1)))
        else:
            ug = jnp.concatenate(ug, axis=0).transpose(1, 0, 2).reshape(width, hidden)
            dg = jnp.concatenate(dg, axis=0).reshape(hidden, width)
            up_grads.append(lax.psum_scatter(ug, "dp", scatter_dimension=1, tiled=True).astype(F32))
            down_grads.append(
                lax.psum_scatter(dg, "dp", scatter_dimension=0, tiled=True).astype(F32)
            )

    flat = lambda parts: [parts[l][m] for m in range(groups) for l in range(local)]
    inputs_grad, grads = vmem_call(
        functools.partial(backward_kernel, experts, local, cap, buckets, shards),
        "attention_backward",
        [shape((n, width)), shape((width, packed.shape[1]))],
        scratch=[
            pltpu.VMEM((n, width), BF16),
            pltpu.VMEM((n, width), F32),
            pltpu.VMEM((width, n), BF16),
            pltpu.VMEM((width, n), BF16),
            pltpu.VMEM((n, width), BF16),
            pltpu.VMEM((n, width), BF16),
            pltpu.VMEM((HEADS, 8, n), F32),
            pltpu.VMEM((LANES, 2 * n), F32),
        ],
        specs=[smem] + [vmem] * (14 + 2 * experts),
        flops=40 * 10**9,
        moved=30 * 10**6,
    )(
        here,
        tokens,
        full,
        routes,
        bucket_row,
        cotangent,
        q,
        k,
        v,
        normed,
        merged_t,
        middle,
        second,
        gates,
        line,
        *flat(backs),
        *flat(dots),
    )
    shares = lax.psum_scatter(grads, "dp", scatter_dimension=0, tiled=True)
    totals = lax.psum(shares, "expert").astype(F32)

    replies = flat([swap_all(r) for r in replies])
    layer_out = vmem_call(
        functools.partial(combine_kernel, local, cap),
        "layer_out",
        shape((n, width)),
        specs=[smem] + [vmem] * (3 + experts),
        flops=4 * n * experts * cap * width,
        moved=6 * 10**6,
    )(here, routes, gates, middle, *replies)

    at = 4 * width
    return (
        layer_out,
        inputs_grad,
        totals[:, :width],
        totals[:, width : 2 * width],
        totals[:, 2 * width : 3 * width],
        totals[:, 3 * width : at],
        totals[:, at : at + experts],
        totals[:, at + experts],
        totals[:, at + experts + 1],
        totals[: bias_table.shape[0], at + TABLE_AT : at + TABLE_AT + HEADS],
        jnp.stack(up_grads),
        jnp.stack(down_grads),
    )


def solution(mesh):
    both, first = P(("dp", "expert"), None), P("dp", None)
    up, down = P("expert", None, "dp"), P("expert", "dp", None)
    return jax.shard_map(
        body,
        mesh=mesh,
        in_specs=(both,)
        + (first,) * 5
        + (P("dp"), P("dp"), first, up, down, both, P(), both),
        out_specs=(both, both) + (first,) * 5 + (P("dp"), P("dp"), first, up, down),
        check_vma=False,
    )
```

time: 963 us -> 548 us (0.57)
  local copies, waits for them, and re-layouts: 299 us -> 21.4 us
  matrix products: 217 us -> 0 us
  Pallas kernels: 0 us -> 143 us
  starting transfers between devices: 20.4 us -> 97.4 us
  blocking collectives: 67.9 us -> 0 us
  other arithmetic: 70.3 us -> 33.9 us
  waiting for transfers between devices: 260 us -> 237 us
    dot_general x40 -> x0, matrix products: 217 us -> none  [the longest x13 88.1 us: product(): return jnp.dot(left, right, preferred_element_type=jnp.float32)]
    ppermute x0 -> x57, waiting for transfers between devices: none -> 203 us  [swap(): lax.ppermute(value, axis, [(i, i ^ bit) for i in range(lax.axis_size(axis...]
    unnamed x155 -> x119, local copies, waits for them, and re-layouts: 166 us -> 8.24 us
    all_to_all x4 -> x0, waiting for transfers between devices: 151 us -> none  [the longest x1 52.3 us: body(): lax.all_to_all(filled.reshape(owners, local_count, capacity, width), 'exp...]
    pallas_call x0 -> x6, Pallas kernels: none -> 143 us  [the longest x4 75.9 us: call(): pl.pallas_call(body, name=name, out_shape=out_shape, in_specs=in_specs, o...]
    reduce_scatter x5 -> x1, waiting for transfers between devices: 105 us -> 0.02 us  [body(): shares = lax.psum_scatter(grads, 'dp', scatter_dimension=0, tiled=True)]
    ppermute x0 -> x57, starting transfers between devices: none -> 97.2 us  [swap(): lax.ppermute(value, axis, [(i, i ^ bit) for i in range(lax.axis_size(axis...]
    reshape x4 -> x0, local copies, waits for them, and re-layouts: 84.8 us -> none  [the longest x1 44.3 us: bias_block(): tiled.reshape(heads, block, period - 1)[:, :, :seq_len].astype(jnp.float32)]
  transfers between devices with their start and end apart: 18 -> 60, of which waited for: 7 -> 25; matrix products, arithmetic and copies ran while one was open for 58% -> 7% of each run, Pallas kernels for 0% -> 18%
where the time goes in v1:
time: 548 us; the launch traced here: 547 us
  waiting for transfers between devices  237 us (43%)
  Pallas kernels  143 us (26%)
  starting transfers between devices  97.4 us (18%)
  other arithmetic  33.9 us (6%)
  local copies, waits for them, and re-layouts  21.4 us (4%)
  between operations  14.6 us (3%)
    ppermute x57, waiting for transfers between devices, swap(): lax.ppermute(value, axis, [(i, i ^ bit) for i in range(lax.axis_size(axis...  203 us
    ppermute x57, starting transfers between devices, swap(): lax.ppermute(value, axis, [(i, i ^ bit) for i in range(lax.axis_size(axis...  97.2 us
    pallas_call x4, Pallas kernels, call(): pl.pallas_call(body, name=name, out_shape=out_shape, in_specs=in_specs, o...  75.9 us
    pallas_call x2, Pallas kernels, body(): pl.pallas_call(functools.partial(expert_kernel, l, groups, cap), name='ex...  66.7 us
    psum x1, waiting for transfers between devices, body(): totals = lax.psum(shares, 'expert').astype(F32)  34.2 us
    concatenate x8, other arithmetic, gather_slabs(): held = jnp.concatenate([held, swap(held, 'dp', bit)], axis=0)  16.8 us
  transfers between devices with their start and end apart: 60, of which 25 were waited for; matrix products, arithmetic and copies ran while one was open for 7% of the time, Pallas kernels for 18%

profile of v1, /device:TPU:0, one launch (start us, length us, event | category | flops | bytes accessed | tf_op | source)
XLA Modules:
  0.0 546.7 jit_solution(1333499834439304019)
XLA Ops:
  12.6 3.0 collective-permute-start.21
  18.8 16.4 %collective-permute-done.21 = bf16[1,768,384]{2,1,0:T(8,128)(2,1)S(1)} collective-permute-done((bf16[1,768,384]{2,1,0:T(8,128)(2,1)S(1)}, bf16[1,768,384]{2,1,0:T(8,128)(2,1)S(1)}, u32[]{:S(2)}, u32[]{:S(2)}) %collective-permute-start.21) | collective-permute-done | bytes 589856 | tf_op jit(solution)/shard_map/ppermute | solution.py:516
  39.3 2.2 collective-permute-start.25
  41.5 10.9 %collective-permute-done.9 = bf16[1,768,384]{2,1,0:T(8,128)(2,1)S(1)} collective-permute-done((bf16[1,768,384]{2,1,0:T(8,128)(2,1)S(1)}, bf16[1,768,384]{2,1,0:T(8,128)(2,1)S(1)}, u32[]{:S(2)}, u32[]{:S(2)}) %collective-permute-start.9) | collective-permute-done | bytes 589856 | tf_op jit(solution)/shard_map/ppermute | solution.py:516
  58.5 3.5 send_cotangent.1
  63.6 26.1 %collective-permute-done.22 = bf16[2,768,384]{2,1,0:T(8,128)(2,1)} collective-permute-done((bf16[2,768,384]{2,1,0:T(8,128)(2,1)}, bf16[2,768,384]{2,1,0:T(8,128)(2,1)}, u32[]{:S(2)}, u32[]{:S(2)}) %collective-permute-start.22) | collective-permute-done | bytes 1179680 | tf_op jit(solution)/shard_map/ppermute | solution.py:516
  89.7 2.6 collective-permute-start.4
  92.3 3.1 pad_maximum_fusion.2.refs_12_
  95.5 3.0 pad_maximum_fusion.3.refs_14_
  99.9 3.5 collective-permute-done.4.refs_6_
  103.4 3.6 collective-permute-start.5
  107.0 6.6 %collective-permute-done.10 = bf16[2,768,384]{2,1,0:T(8,128)(2,1)} collective-permute-done((bf16[2,768,384]{2,1,0:T(8,128)(2,1)}, bf16[2,768,384]{2,1,0:T(8,128)(2,1)}, u32[]{:S(2)}, u32[]{:S(2)}) %collective-permute-start.10) | collective-permute-done | bytes 1179680 | tf_op jit(solution)/shard_map/ppermute | solution.py:516
  115.1 2.6 collective-permute-start.19
  117.7 3.0 pad_maximum_fusion.refs_12_
  120.7 3.0 pad_maximum_fusion.1.refs_14_
  123.9 2.5 collective-permute-done.18.refs_5_
  126.4 12.3 %collective-permute-done.19.refs_6_ = bf16[192,768]{1,0:T(8,128)(2,1)S(1)} collective-permute-done((bf16[192,768]{1,0:T(8,128)(2,1)}, bf16[192,768]{1,0:T(8,128)(2,1)S(1)}, u32[]{:S(2)}, u32[]{:S(2)}) %collective-permute-start.19) | collective-permute-done | bytes 294944 | tf_op jit(solution)/shard_map/ppermute | solution.py:516
  138.7 20.3 %attention_forward.1 = (bf16[512,768]{1,0:T(8,128)(2,1)}, bf16[512,768]{1,0:T(8,128)(2,1)}, bf16[512,768]{1,0:T(8,128)(2,1)}, bf16[512,768]{1,0:T(8,128)(2,1)}, ...) custom-call(s32[1]{0:T(128)} %bitcast.here_ref, ...), custom_call_target="tpu_custom_call" | custom-call | flops 20000000000 | bytes 20000000 | tf_op jit(solution)/shard_map/attention_forward/pallas_call | solution.py:47
  159.1 2.5 collective-permute-start.7
  164.0 2.4 collective-permute-start.16
  169.4 8.2 %collective-permute-done.15.refs_1_ = bf16[192,768]{1,0:T(8,128)(2,1)S(1)} collective-permute-done((bf16[192,768]{1,0:T(8,128)(2,1)}, bf16[192,768]{1,0:T(8,128)(2,1)S(1)}, u32[]{:S(2)}, u32[]{:S(2)}) %collective-permute-start.15) | collective-permute-done | bytes 294944 | tf_op jit(solution)/shard_map/ppermute | solution.py:516
  177.5 10.2 %collective-permute-done.16.refs_2_ = bf16[192,768]{1,0:T(8,128)(2,1)S(1)} collective-permute-done((bf16[192,768]{1,0:T(8,128)(2,1)}, bf16[192,768]{1,0:T(8,128)(2,1)S(1)}, u32[]{:S(2)}, u32[]{:S(2)}) %collective-permute-start.16) | collective-permute-done | bytes 294944 | tf_op jit(solution)/shard_map/ppermute | solution.py:516
  191.1 33.3 %expert.3 = (bf16[192,768]{1,0:T(8,128)(2,1)}, bf16[192,768]{1,0:T(8,128)(2,1)}, bf16[192,768]{1,0:T(8,128)(2,1)}, bf16[192,768]{1,0:T(8,128)(2,1)}, bf16[192,76...) custom-call(bf16[192,768]{1,0:T(8,128)(2,1)} %get-tuple-element.90.r, ...), custom_call_target="tpu_custom_call" | custom-call | flops 21743271936 | bytes 40000000 | tf_op jit(solution)/shard_map/expert/pallas_call | solution.py:650
  224.4 18.0 %collective-permute-start.34 = (bf16[192,768]{1,0:T(8,128)(2,1)}, bf16[192,768]{1,0:T(8,128)(2,1)S(1)}, u32[]{:S(2)}, u32[]{:S(2)}) collective-permute-start(bf16[192,768]{1,0:T(8,128)(2,1)} %get-tuple-element.115), channel_id=1, source_target_pairs={{0,1},{1,0},{2,3},{3,2},{4,5},{5,4},{6,7},{7,6},{8,9},{9,8},{10,11... | collective-permute-start | bytes 884744 | tf_op jit(solution)/shard_map/ppermute | solution.py:516
  242.5 2.3 collective-permute-start.42
  247.5 33.4 %expert.2 = (bf16[192,768]{1,0:T(8,128)(2,1)}, bf16[192,768]{1,0:T(8,128)(2,1)}, bf16[192,768]{1,0:T(8,128)(2,1)}, bf16[192,768]{1,0:T(8,128)(2,1)}, bf16[192,76...) custom-call(bf16[192,768]{1,0:T(8,128)(2,1)} %get-tuple-element.77.r, ...), custom_call_target="tpu_custom_call" | custom-call | flops 21743271936 | bytes 40000000 | tf_op jit(solution)/shard_map/expert/pallas_call | solution.py:650
  281.1 2.4 collective-permute-start.41
  291.9 16.4 %collective-permute-done.36.rest_5_ = bf16[192,768]{1,0:T(8,128)(2,1)S(1)} collective-permute-done((bf16[192,768]{1,0:T(8,128)(2,1)S(1)}, bf16[192,768]{1,0:T(8,128)(2,1)S(1)}, u32[]{:S(2)}, u32[]{:S(2)}) %collective-permute-start.36) | collective-permute-done | bytes 294944 | tf_op jit(solution)/shard_map/ppermute | solution.py:516
  308.3 10.3 %collective-permute-done.35.rest_4_ = bf16[192,768]{1,0:T(8,128)(2,1)S(1)} collective-permute-done((bf16[192,768]{1,0:T(8,128)(2,1)}, bf16[192,768]{1,0:T(8,128)(2,1)S(1)}, u32[]{:S(2)}, u32[]{:S(2)}) %collective-permute-start.35) | collective-permute-done | bytes 294944 | tf_op jit(solution)/shard_map/ppermute | solution.py:516
  319.4 44.8 %attention_backward.1 = (bf16[512,768]{1,0:T(8,128)(2,1)}, bf16[768,3200]{1,0:T(8,128)(2,1)}) custom-call(s32[1]{0:T(128)} %bitcast.here_ref, bf16[512,768]{1,0:T(8,128)(2,1)} %tok_ref.3, bf16[768,3200]{1,0:T(8,128)(2,1)} %all-gather.2.cloned.1.call-done.w_ref, s32[512,2]{1,0:T(8,128)} %copy.37.routes_ref, s32[1,512]{1,0:T(1,128)} %bitcast.10, ...), custom_call_target="tpu_custom_call" | custom-call | flops 40000000000 | bytes 30000000 | tf_op jit(solution)/shard_map/attention_backward/pallas_call | solution.py:47
  366.9 3.6 collective-permute-start.28
  370.5 3.2 collective-permute-done.51
  373.8 3.8 collective-permute-start.30
  377.6 2.2 add_convert_fusion.1
  380.9 2.2 collective-permute-start.52
  386.3 11.7 %collective-permute-done.30.rest_5_ = bf16[192,768]{1,0:T(8,128)(2,1)S(1)} collective-permute-done((bf16[192,768]{1,0:T(8,128)(2,1)S(1)}, bf16[192,768]{1,0:T(8,128)(2,1)S(1)}, u32[]{:S(2)}, u32[]{:S(2)}) %collective-permute-start.30) | collective-permute-done | bytes 294944 | tf_op jit(solution)/shard_map/ppermute | solution.py:516
  398.0 2.3 collective-permute-start.55
  402.1 3.0 collective-permute-start.29
  405.1 2.4 collective-permute-done.27.rest_2_
  407.5 2.7 collective-permute-start.31
  414.1 11.6 %collective-permute-done.29.rest_4_ = bf16[192,768]{1,0:T(8,128)(2,1)S(1)} collective-permute-done((bf16[192,768]{1,0:T(8,128)(2,1)S(1)}, bf16[192,768]{1,0:T(8,128)(2,1)S(1)}, u32[]{:S(2)}, u32[]{:S(2)}) %collective-permute-start.29) | collective-permute-done | bytes 294944 | tf_op jit(solution)/shard_map/ppermute | solution.py:516
  427.9 7.3 %layer_out.1 = bf16[512,768]{1,0:T(8,128)(2,1)} custom-call(s32[1]{0:T(128)} %bitcast.here_ref, s32[512,2]{1,0:T(8,128)} %copy.37.routes_ref, f32[512,128]{1,0:T(8,128)} %get-tuple-element.75.gates_ref, f32[512,768]{1,0:T(8,128)} %get-tuple-element.76.middle_ref, bf16[192,768]{1,0:T(8,128)(2,1)} %get-tuple-element.89.rest_0_, ...), custom_call_target="tpu_custom_call" | custom-call | flops 2415919104 | bytes 6000000 | tf_op jit(solution)/shard_map/layer_out/pallas_call | solution.py:47
  436.3 18.1 %collective-permute-done.55 = bf16[2,384,768]{2,1,0:T(8,128)(2,1)} collective-permute-done((bf16[2,384,768]{2,1,0:T(8,128)(2,1)}, bf16[2,384,768]{2,1,0:T(8,128)(2,1)}, u32[]{:S(2)}, u32[]{:S(2)}) %collective-permute-start.55) | collective-permute-done | bytes 1179680 | tf_op jit(solution)/shard_map/ppermute | solution.py:516
  461.1 10.1 %collective-permute-done.49 = bf16[2,768,384]{2,1,0:T(8,128)(2,1)} collective-permute-done((bf16[2,768,384]{2,1,0:T(8,128)(2,1)}, bf16[2,768,384]{2,1,0:T(8,128)(2,1)}, u32[]{:S(2)}, u32[]{:S(2)}) %collective-permute-start.49) | collective-permute-done | bytes 1179680 | tf_op jit(solution)/shard_map/ppermute | solution.py:516
  474.5 9.3 %collective-permute-done.53 = bf16[1,384,768]{2,1,0:T(8,128)(2,1)S(1)} collective-permute-done((bf16[1,384,768]{2,1,0:T(8,128)(2,1)S(1)}, bf16[1,384,768]{2,1,0:T(8,128)(2,1)S(1)}, u32[]{:S(2)}, u32[]{:S(2)}) %collective-permute-start.53) | collective-permute-done | bytes 589856 | tf_op jit(solution)/shard_map/ppermute | solution.py:516
  483.9 10.0 %collective-permute-done.56 = bf16[1,384,768]{2,1,0:T(8,128)(2,1)S(1)} collective-permute-done((bf16[1,384,768]{2,1,0:T(8,128)(2,1)S(1)}, bf16[1,384,768]{2,1,0:T(8,128)(2,1)S(1)}, u32[]{:S(2)}, u32[]{:S(2)}) %collective-permute-start.56) | collective-permute-done | bytes 589856 | tf_op jit(solution)/shard_map/ppermute | solution.py:516
  495.2 2.8 pad_maximum_fusion.5
  500.8 34.2 %all-reduce.3.cloned.1.call-done = bf16[96,3200]{1,0:T(8,128)(2,1)} async-done(((bf16[96,3200]{1,0:T(8,128)(2,1)}), bf16[96,3200]{1,0:T(8,128)(2,1)}) %all-reduce.3.cloned.1.call-update) | async-done | bytes 614416 | tf_op jit(solution)/shard_map/psum | solution.py:733
  (243 shorter events, 79.3 us)
Async XLA Ops:
  7.2 131.5 %all-gather.2.cloned.1.call-start = ((), (), s32[]{:S(2)}) async-start(), calls=%async_computation.1 | async-start | bytes 5529600 | tf_op jit(solution)/shard_map/all_gather | solution.py:591
  12.4 482.9 %reduce-scatter.2.cloned.1.call-start = ((), (), s32[]{:S(2)}) async-start(), calls=%async_computation.2 | async-start | bytes 5529600 | tf_op jit(solution)/shard_map/reduce_scatter | solution.py:732
  12.6 22.6 %collective-permute-start.21 = (bf16[1,768,384]{2,1,0:T(8,128)(2,1)S(1)}, bf16[1,768,384]{2,1,0:T(8,128)(2,1)S(1)}, u32[]{:S(2)}, u32[]{:S(2)}) collective-permute-start(bf16[1,768,384]{2,1,0:T(8,128)(2,1)S(1)} %get-tuple-element.166), channel_id=1, source_target_pairs={{0,8},{4,12},{8,0},{12,4},{16,24},{20,28},{24,16},{28,20},{1,9},{5... | collective-permute-start | bytes 1769480 | tf_op jit(solution)/shard_map/ppermute | solution.py:516
  15.6 22.4 %collective-permute-start.24 = (bf16[1,384,768]{2,1,0:T(8,128)(2,1)S(1)}, bf16[1,384,768]{2,1,0:T(8,128)(2,1)S(1)}, u32[]{:S(2)}, u32[]{:S(2)}) collective-permute-start(bf16[1,384,768]{2,1,0:T(8,128)(2,1)S(1)} %get-tuple-element.164), channel_id=1, source_target_pairs={{0,16},{4,20},{8,24},{12,28},{16,0},{20,4},{24,8},{28,12},{1,17},{... | collective-permute-start | bytes 1769480 | tf_op jit(solution)/shard_map/ppermute | solution.py:516
  17.2 35.1 %collective-permute-start.9 = (bf16[1,768,384]{2,1,0:T(8,128)(2,1)S(1)}, bf16[1,768,384]{2,1,0:T(8,128)(2,1)S(1)}, u32[]{:S(2)}, u32[]{:S(2)}) collective-permute-start(bf16[1,768,384]{2,1,0:T(8,128)(2,1)S(1)} %get-tuple-element.167), channel_id=1, source_target_pairs={{0,8},{4,12},{8,0},{12,4},{16,24},{20,28},{24,16},{28,20},{1,9},{5... | collective-permute-start | bytes 1769480 | tf_op jit(solution)/shard_map/ppermute | solution.py:516
  18.3 37.5 %collective-permute-start.12 = (bf16[1,384,768]{2,1,0:T(8,128)(2,1)S(1)}, bf16[1,384,768]{2,1,0:T(8,128)(2,1)S(1)}, u32[]{:S(2)}, u32[]{:S(2)}) collective-permute-start(bf16[1,384,768]{2,1,0:T(8,128)(2,1)S(1)} %get-tuple-element.165), channel_id=1, source_target_pairs={{0,16},{4,20},{8,24},{12,28},{16,0},{20,4},{24,8},{28,12},{1,17},{... | collective-permute-start | bytes 1769480 | tf_op jit(solution)/shard_map/ppermute | solution.py:516
  36.4 53.4 %collective-permute-start.22 = (bf16[2,768,384]{2,1,0:T(8,128)(2,1)}, bf16[2,768,384]{2,1,0:T(8,128)(2,1)}, u32[]{:S(2)}, u32[]{:S(2)}) collective-permute-start(bf16[2,768,384]{2,1,0:T(8,128)(2,1)} %pad_maximum_fusion.8), channel_id=1, source_target_pairs={{0,16},{4,20},{8,24},{12,28},{16,0},{20,4},{24,8},{28,12},{1,17},{... | collective-permute-start | bytes 3538952 | tf_op jit(solution)/shard_map/ppermute | solution.py:516
  39.3 56.2 %collective-permute-start.25 = (bf16[2,384,768]{2,1,0:T(8,128)(2,1)}, bf16[2,384,768]{2,1,0:T(8,128)(2,1)}, u32[]{:S(2)}, u32[]{:S(2)}) collective-permute-start(bf16[2,384,768]{2,1,0:T(8,128)(2,1)} %pad_maximum_fusion.9), channel_id=1, source_target_pairs={{0,8},{4,12},{8,0},{12,4},{16,24},{20,28},{24,16},{28,20},{1,9},{5... | collective-permute-start | bytes 3538952 | tf_op jit(solution)/shard_map/ppermute | solution.py:516
  53.5 60.1 %collective-permute-start.10 = (bf16[2,768,384]{2,1,0:T(8,128)(2,1)}, bf16[2,768,384]{2,1,0:T(8,128)(2,1)}, u32[]{:S(2)}, u32[]{:S(2)}) collective-permute-start(bf16[2,768,384]{2,1,0:T(8,128)(2,1)} %pad_maximum_fusion.6), channel_id=1, source_target_pairs={{0,16},{4,20},{8,24},{12,28},{16,0},{20,4},{24,8},{28,12},{1,17},{... | collective-permute-start | bytes 3538952 | tf_op jit(solution)/shard_map/ppermute | solution.py:516
  57.0 58.2 %collective-permute-start.13 = (bf16[2,384,768]{2,1,0:T(8,128)(2,1)}, bf16[2,384,768]{2,1,0:T(8,128)(2,1)}, u32[]{:S(2)}, u32[]{:S(2)}) collective-permute-start(bf16[2,384,768]{2,1,0:T(8,128)(2,1)} %pad_maximum_fusion.7), channel_id=1, source_target_pairs={{0,8},{4,12},{8,0},{12,4},{16,24},{20,28},{24,16},{28,20},{1,9},{5... | collective-permute-start | bytes 3538952 | tf_op jit(solution)/shard_map/ppermute | solution.py:516
  62.0 36.6 %collective-permute-start.3 = (bf16[192,768]{1,0:T(8,128)(2,1)}, bf16[192,768]{1,0:T(8,128)(2,1)}, u32[]{:S(2)}, u32[]{:S(2)}) collective-permute-start(bf16[192,768]{1,0:T(8,128)(2,1)} %get-tuple-element.82), channel_id=1, source_target_pairs={{0,1},{1,0},{2,3},{3,2},{4,5},{5,4},{6,7},{7,6},{8,9},{9,8},{10,11... | collective-permute-start | bytes 884744 | tf_op jit(solution)/shard_map/ppermute | solution.py:516
  95.5 63.7 %collective-permute-start.23 = (bf16[4,768,384]{2,1,0:T(8,128)(2,1)}, bf16[4,768,384]{2,1,0:T(8,128)(2,1)}, u32[]{:S(2)}, u32[]{:S(2)}) collective-permute-start(bf16[4,768,384]{2,1,0:T(8,128)(2,1)} %pad_maximum_fusion.2.refs_12_), channel_id=1, source_target_pairs={{0,4},{4,0},{8,12},{12,8},{16,20},{20,16},{24,28},{28,24},{1,5},{5... | collective-permute-start | bytes 7077896 | tf_op jit(solution)/shard_map/ppermute | solution.py:516
  98.6 63.1 %collective-permute-start.26 = (bf16[4,384,768]{2,1,0:T(8,128)(2,1)}, bf16[4,384,768]{2,1,0:T(8,128)(2,1)}, u32[]{:S(2)}, u32[]{:S(2)}) collective-permute-start(bf16[4,384,768]{2,1,0:T(8,128)(2,1)} %pad_maximum_fusion.3.refs_14_), channel_id=1, source_target_pairs={{0,4},{4,0},{8,12},{12,8},{16,20},{20,16},{24,28},{28,24},{1,5},{5... | collective-permute-start | bytes 7077896 | tf_op jit(solution)/shard_map/ppermute | solution.py:516
  103.4 20.3 %collective-permute-start.5 = (bf16[192,768]{1,0:T(8,128)(2,1)S(1)}, bf16[192,768]{1,0:T(8,128)(2,1)S(1)}, u32[]{:S(2)}, u32[]{:S(2)}) collective-permute-start(bf16[192,768]{1,0:T(8,128)(2,1)S(1)} %copy-done.36), channel_id=1, source_target_pairs={{0,3},{1,2},{2,1},{3,0},{4,7},{5,6},{6,5},{7,4},{8,11},{9,10},{10,... | collective-permute-start | bytes 884744 | tf_op jit(solution)/shard_map/ppermute | solution.py:516
  115.1 23.5 %collective-permute-start.19 = (bf16[192,768]{1,0:T(8,128)(2,1)}, bf16[192,768]{1,0:T(8,128)(2,1)S(1)}, u32[]{:S(2)}, u32[]{:S(2)}) collective-permute-start(bf16[192,768]{1,0:T(8,128)(2,1)} %get-tuple-element.96), channel_id=1, source_target_pairs={{0,2},{1,3},{2,0},{3,1},{4,6},{5,7},{6,4},{7,5},{8,10},{9,11},{10,... | collective-permute-start | bytes 884744 | tf_op jit(solution)/shard_map/ppermute | solution.py:516
  123.7 35.4 %collective-permute-start.20 = (bf16[192,768]{1,0:T(8,128)(2,1)}, bf16[192,768]{1,0:T(8,128)(2,1)S(1)}, u32[]{:S(2)}, u32[]{:S(2)}) collective-permute-start(bf16[192,768]{1,0:T(8,128)(2,1)} %get-tuple-element.97), channel_id=1, source_target_pairs={{0,3},{1,2},{2,1},{3,0},{4,7},{5,6},{6,5},{7,4},{8,11},{9,10},{10,... | collective-permute-start | bytes 884744 | tf_op jit(solution)/shard_map/ppermute | solution.py:516
  126.4 98.1 %collective-permute-start.11 = (bf16[4,768,384]{2,1,0:T(8,128)(2,1)}, bf16[4,768,384]{2,1,0:T(8,128)(2,1)S(1)}, u32[]{:S(2)}, u32[]{:S(2)}) collective-permute-start(bf16[4,768,384]{2,1,0:T(8,128)(2,1)} %pad_maximum_fusion.refs_12_), channel_id=1, source_target_pairs={{0,4},{4,0},{8,12},{12,8},{16,20},{20,16},{24,28},{28,24},{1,5},{5... | collective-permute-start | bytes 7077896 | tf_op jit(solution)/shard_map/ppermute | solution.py:516
  138.7 103.7 %collective-permute-start.14 = (bf16[4,384,768]{2,1,0:T(8,128)(2,1)}, bf16[4,384,768]{2,1,0:T(8,128)(2,1)}, u32[]{:S(2)}, u32[]{:S(2)}) collective-permute-start(bf16[4,384,768]{2,1,0:T(8,128)(2,1)} %pad_maximum_fusion.1.refs_14_), channel_id=1, source_target_pairs={{0,4},{4,0},{8,12},{12,8},{16,20},{20,16},{24,28},{28,24},{1,5},{5... | collective-permute-start | bytes 7077896 | tf_op jit(solution)/shard_map/ppermute | solution.py:516
  164.0 23.7 %collective-permute-start.16 = (bf16[192,768]{1,0:T(8,128)(2,1)}, bf16[192,768]{1,0:T(8,128)(2,1)S(1)}, u32[]{:S(2)}, u32[]{:S(2)}) collective-permute-start(bf16[192,768]{1,0:T(8,128)(2,1)} %get-tuple-element.92), channel_id=1, source_target_pairs={{0,2},{1,3},{2,0},{3,1},{4,6},{5,7},{6,4},{7,5},{8,10},{9,11},{10,... | collective-permute-start | bytes 884744 | tf_op jit(solution)/shard_map/ppermute | solution.py:516
  167.5 20.9 %collective-permute-start.17 = (bf16[192,768]{1,0:T(8,128)(2,1)}, bf16[192,768]{1,0:T(8,128)(2,1)S(1)}, u32[]{:S(2)}, u32[]{:S(2)}) collective-permute-start(bf16[192,768]{1,0:T(8,128)(2,1)} %get-tuple-element.93), channel_id=1, source_target_pairs={{0,3},{1,2},{2,1},{3,0},{4,7},{5,6},{6,5},{7,4},{8,11},{9,10},{10,... | collective-permute-start | bytes 884744 | tf_op jit(solution)/shard_map/ppermute | solution.py:516
  177.5 65.0 %collective-permute-start = (bf16[192,768]{1,0:T(8,128)(2,1)}, bf16[192,768]{1,0:T(8,128)(2,1)S(1)}, u32[]{:S(2)}, u32[]{:S(2)}) collective-permute-start(bf16[192,768]{1,0:T(8,128)(2,1)} %get-tuple-element.78), channel_id=1, source_target_pairs={{0,1},{1,0},{2,3},{3,2},{4,5},{5,4},{6,7},{7,6},{8,9},{9,8},{10,11... | collective-permute-start | bytes 884744 | tf_op jit(solution)/shard_map/ppermute | solution.py:516
  188.4 56.4 %collective-permute-start.1 = (bf16[192,768]{1,0:T(8,128)(2,1)}, bf16[192,768]{1,0:T(8,128)(2,1)S(1)}, u32[]{:S(2)}, u32[]{:S(2)}) collective-permute-start(bf16[192,768]{1,0:T(8,128)(2,1)} %get-tuple-element.79), channel_id=1, source_target_pairs={{0,2},{1,3},{2,0},{3,1},{4,6},{5,7},{6,4},{7,5},{8,10},{9,11},{10,... | collective-permute-start | bytes 884744 | tf_op jit(solution)/shard_map/ppermute | solution.py:516
  189.1 57.7 %collective-permute-start.2 = (bf16[192,768]{1,0:T(8,128)(2,1)}, bf16[192,768]{1,0:T(8,128)(2,1)S(1)}, u32[]{:S(2)}, u32[]{:S(2)}) collective-permute-start(bf16[192,768]{1,0:T(8,128)(2,1)} %get-tuple-element.80), channel_id=1, source_target_pairs={{0,3},{1,2},{2,1},{3,0},{4,7},{5,6},{6,5},{7,4},{8,11},{9,10},{10,... | collective-permute-start | bytes 884744 | tf_op jit(solution)/shard_map/ppermute | solution.py:516
  224.4 65.6 %collective-permute-start.34 = (bf16[192,768]{1,0:T(8,128)(2,1)}, bf16[192,768]{1,0:T(8,128)(2,1)S(1)}, u32[]{:S(2)}, u32[]{:S(2)}) collective-permute-start(bf16[192,768]{1,0:T(8,128)(2,1)} %get-tuple-element.115), channel_id=1, source_target_pairs={{0,1},{1,0},{2,3},{3,2},{4,5},{5,4},{6,7},{7,6},{8,9},{9,8},{10,11... | collective-permute-start | bytes 884744 | tf_op jit(solution)/shard_map/ppermute | solution.py:516
  242.4 38.6 %collective-permute-start.40 = (f32[8,256]{1,0:T(8,128)}, f32[8,256]{1,0:T(8,128)S(1)}, u32[]{:S(2)}, u32[]{:S(2)}) collective-permute-start(f32[8,256]{1,0:T(8,128)} %get-tuple-element.123), channel_id=1, source_target_pairs={{0,1},{1,0},{2,3},{3,2},{4,5},{5,4},{6,7},{7,6},{8,9},{9,8},{10,11... | collective-permute-start | bytes 24584 | tf_op jit(solution)/shard_map/ppermute | solution.py:516
  242.5 41.0 %collective-permute-start.42 = (f32[8,256]{1,0:T(8,128)}, f32[8,256]{1,0:T(8,128)S(1)}, u32[]{:S(2)}, u32[]{:S(2)}) collective-permute-start(f32[8,256]{1,0:T(8,128)} %get-tuple-element.125), channel_id=1, source_target_pairs={{0,2},{1,3},{2,0},{3,1},{4,6},{5,7},{6,4},{7,5},{8,10},{9,11},{10,... | collective-permute-start | bytes 24584 | tf_op jit(solution)/shard_map/ppermute | solution.py:516
  244.8 40.6 %collective-permute-start.44 = (f32[8,256]{1,0:T(8,128)}, f32[8,256]{1,0:T(8,128)S(1)}, u32[]{:S(2)}, u32[]{:S(2)}) collective-permute-start(f32[8,256]{1,0:T(8,128)} %get-tuple-element.127), channel_id=1, source_target_pairs={{0,3},{1,2},{2,1},{3,0},{4,7},{5,6},{6,5},{7,4},{8,11},{9,10},{10,... | collective-permute-start | bytes 24584 | tf_op jit(solution)/shard_map/ppermute | solution.py:516
  285.4 22.8 %collective-permute-start.36 = (bf16[192,768]{1,0:T(8,128)(2,1)S(1)}, bf16[192,768]{1,0:T(8,128)(2,1)S(1)}, u32[]{:S(2)}, u32[]{:S(2)}) collective-permute-start(bf16[192,768]{1,0:T(8,128)(2,1)S(1)} %copy-done.28), channel_id=1, source_target_pairs={{0,2},{1,3},{2,0},{3,1},{4,6},{5,7},{6,4},{7,5},{8,10},{9,11},{10,... | collective-permute-start | bytes 884744 | tf_op jit(solution)/shard_map/ppermute | solution.py:516
  285.5 22.7 %collective-permute-start.38 = (bf16[192,768]{1,0:T(8,128)(2,1)S(1)}, bf16[192,768]{1,0:T(8,128)(2,1)S(1)}, u32[]{:S(2)}, u32[]{:S(2)}) collective-permute-start(bf16[192,768]{1,0:T(8,128)(2,1)S(1)} %copy-done.26), channel_id=1, source_target_pairs={{0,3},{1,2},{2,1},{3,0},{4,7},{5,6},{6,5},{7,4},{8,11},{9,10},{10,... | collective-permute-start | bytes 884744 | tf_op jit(solution)/shard_map/ppermute | solution.py:516
  287.5 20.8 %collective-permute-start.33 = (bf16[192,768]{1,0:T(8,128)(2,1)}, bf16[192,768]{1,0:T(8,128)(2,1)S(1)}, u32[]{:S(2)}, u32[]{:S(2)}) collective-permute-start(bf16[192,768]{1,0:T(8,128)(2,1)} %get-tuple-element.114), channel_id=1, source_target_pairs={{0,1},{1,0},{2,3},{3,2},{4,5},{5,4},{6,7},{7,6},{8,9},{9,8},{10,11... | collective-permute-start | bytes 884744 | tf_op jit(solution)/shard_map/ppermute | solution.py:516
  289.2 29.4 %collective-permute-start.35 = (bf16[192,768]{1,0:T(8,128)(2,1)}, bf16[192,768]{1,0:T(8,128)(2,1)S(1)}, u32[]{:S(2)}, u32[]{:S(2)}) collective-permute-start(bf16[192,768]{1,0:T(8,128)(2,1)} %get-tuple-element.116), channel_id=1, source_target_pairs={{0,2},{1,3},{2,0},{3,1},{4,6},{5,7},{6,4},{7,5},{8,10},{9,11},{10,... | collective-permute-start | bytes 884744 | tf_op jit(solution)/shard_map/ppermute | solution.py:516
  290.0 28.6 %collective-permute-start.37 = (bf16[192,768]{1,0:T(8,128)(2,1)}, bf16[192,768]{1,0:T(8,128)(2,1)S(1)}, u32[]{:S(2)}, u32[]{:S(2)}) collective-permute-start(bf16[192,768]{1,0:T(8,128)(2,1)} %get-tuple-element.118), channel_id=1, source_target_pairs={{0,3},{1,2},{2,1},{3,0},{4,7},{5,6},{6,5},{7,4},{8,11},{9,10},{10,... | collective-permute-start | bytes 884744 | tf_op jit(solution)/shard_map/ppermute | solution.py:516
  364.3 170.7 %all-reduce.3.cloned.1.call-start = ((), (), s32[]{:S(2)}) async-start(), calls=%async_computation.3 | async-start | bytes 1228800 | tf_op jit(solution)/shard_map/psum | solution.py:733
  366.4 31.6 %collective-permute-start.45 = (bf16[4,768,384]{2,1,0:T(8,128)(2,1)}, bf16[4,768,384]{2,1,0:T(8,128)(2,1)S(1)}, u32[]{:S(2)}, u32[]{:S(2)}) collective-permute-start(bf16[4,768,384]{2,1,0:T(8,128)(2,1)} %get-tuple-element.131), channel_id=1, source_target_pairs={{0,4},{4,0},{8,12},{12,8},{16,20},{20,16},{24,28},{28,24},{1,5},{5... | collective-permute-start | bytes 7077896 | tf_op jit(solution)/shard_map/ppermute | solution.py:516
  366.4 43.8 %collective-permute-start.48 = (bf16[4,768,384]{2,1,0:T(8,128)(2,1)}, bf16[4,768,384]{2,1,0:T(8,128)(2,1)S(1)}, u32[]{:S(2)}, u32[]{:S(2)}) collective-permute-start(bf16[4,768,384]{2,1,0:T(8,128)(2,1)} %get-tuple-element.133), channel_id=1, source_target_pairs={{0,4},{4,0},{8,12},{12,8},{16,20},{20,16},{24,28},{28,24},{1,5},{5... | collective-permute-start | bytes 7077896 | tf_op jit(solution)/shard_map/ppermute | solution.py:516
  366.9 17.9 %collective-permute-start.28 = (bf16[192,768]{1,0:T(8,128)(2,1)S(1)}, bf16[192,768]{1,0:T(8,128)(2,1)S(1)}, u32[]{:S(2)}, u32[]{:S(2)}) collective-permute-start(bf16[192,768]{1,0:T(8,128)(2,1)S(1)} %copy-done.20), channel_id=1, source_target_pairs={{0,1},{1,0},{2,3},{3,2},{4,5},{5,4},{6,7},{7,6},{8,9},{9,8},{10,11... | collective-permute-start | bytes 884744 | tf_op jit(solution)/shard_map/ppermute | solution.py:516
  373.8 24.3 %collective-permute-start.30 = (bf16[192,768]{1,0:T(8,128)(2,1)S(1)}, bf16[192,768]{1,0:T(8,128)(2,1)S(1)}, u32[]{:S(2)}, u32[]{:S(2)}) collective-permute-start(bf16[192,768]{1,0:T(8,128)(2,1)S(1)} %copy-done.19), channel_id=1, source_target_pairs={{0,2},{1,3},{2,0},{3,1},{4,6},{5,7},{6,4},{7,5},{8,10},{9,11},{10,... | collective-permute-start | bytes 884744 | tf_op jit(solution)/shard_map/ppermute | solution.py:516
  380.9 54.3 %collective-permute-start.52 = (bf16[2,384,768]{2,1,0:T(8,128)(2,1)}, bf16[2,384,768]{2,1,0:T(8,128)(2,1)S(1)}, u32[]{:S(2)}, u32[]{:S(2)}) collective-permute-start(bf16[2,384,768]{2,1,0:T(8,128)(2,1)} %slice.129), channel_id=1, source_target_pairs={{0,8},{4,12},{8,0},{12,4},{16,24},{20,28},{24,16},{28,20},{1,9},{5... | collective-permute-start | bytes 3538952 | tf_op jit(solution)/shard_map/ppermute | solution.py:516
  384.8 17.3 %collective-permute-start.32 = (bf16[192,768]{1,0:T(8,128)(2,1)S(1)}, bf16[192,768]{1,0:T(8,128)(2,1)S(1)}, u32[]{:S(2)}, u32[]{:S(2)}) collective-permute-start(bf16[192,768]{1,0:T(8,128)(2,1)S(1)} %copy-done.18), channel_id=1, source_target_pairs={{0,3},{1,2},{2,1},{3,0},{4,7},{5,6},{6,5},{7,4},{8,11},{9,10},{10,... | collective-permute-start | bytes 884744 | tf_op jit(solution)/shard_map/ppermute | solution.py:516
  398.0 56.4 %collective-permute-start.55 = (bf16[2,384,768]{2,1,0:T(8,128)(2,1)}, bf16[2,384,768]{2,1,0:T(8,128)(2,1)}, u32[]{:S(2)}, u32[]{:S(2)}) collective-permute-start(bf16[2,384,768]{2,1,0:T(8,128)(2,1)} %slice.133), channel_id=1, source_target_pairs={{0,8},{4,12},{8,0},{12,4},{16,24},{20,28},{24,16},{28,20},{1,9},{5... | collective-permute-start | bytes 3538952 | tf_op jit(solution)/shard_map/ppermute | solution.py:516
  402.1 23.6 %collective-permute-start.29 = (bf16[192,768]{1,0:T(8,128)(2,1)S(1)}, bf16[192,768]{1,0:T(8,128)(2,1)S(1)}, u32[]{:S(2)}, u32[]{:S(2)}) collective-permute-start(bf16[192,768]{1,0:T(8,128)(2,1)S(1)} %copy-done.22), channel_id=1, source_target_pairs={{0,2},{1,3},{2,0},{3,1},{4,6},{5,7},{6,4},{7,5},{8,10},{9,11},{10,... | collective-permute-start | bytes 884744 | tf_op jit(solution)/shard_map/ppermute | solution.py:516
  407.5 19.7 %collective-permute-start.31 = (bf16[192,768]{1,0:T(8,128)(2,1)S(1)}, bf16[192,768]{1,0:T(8,128)(2,1)S(1)}, u32[]{:S(2)}, u32[]{:S(2)}) collective-permute-start(bf16[192,768]{1,0:T(8,128)(2,1)S(1)} %copy-done.21), channel_id=1, source_target_pairs={{0,3},{1,2},{2,1},{3,0},{4,7},{5,6},{6,5},{7,4},{8,11},{9,10},{10,... | collective-permute-start | bytes 884744 | tf_op jit(solution)/shard_map/ppermute | solution.py:516
  410.2 47.5 %collective-permute-start.46 = (bf16[2,768,384]{2,1,0:T(8,128)(2,1)}, bf16[2,768,384]{2,1,0:T(8,128)(2,1)}, u32[]{:S(2)}, u32[]{:S(2)}) collective-permute-start(bf16[2,768,384]{2,1,0:T(8,128)(2,1)} %slice.121), channel_id=1, source_target_pairs={{0,16},{4,20},{8,24},{12,28},{16,0},{20,4},{24,8},{28,12},{1,17},{... | collective-permute-start | bytes 3538952 | tf_op jit(solution)/shard_map/ppermute | solution.py:516
  425.7 45.6 %collective-permute-start.49 = (bf16[2,768,384]{2,1,0:T(8,128)(2,1)}, bf16[2,768,384]{2,1,0:T(8,128)(2,1)}, u32[]{:S(2)}, u32[]{:S(2)}) collective-permute-start(bf16[2,768,384]{2,1,0:T(8,128)(2,1)} %slice.125), channel_id=1, source_target_pairs={{0,16},{4,20},{8,24},{12,28},{16,0},{20,4},{24,8},{28,12},{1,17},{... | collective-permute-start | bytes 3538952 | tf_op jit(solution)/shard_map/ppermute | solution.py:516
  435.5 48.3 %collective-permute-start.53 = (bf16[1,384,768]{2,1,0:T(8,128)(2,1)S(1)}, bf16[1,384,768]{2,1,0:T(8,128)(2,1)S(1)}, u32[]{:S(2)}, u32[]{:S(2)}) collective-permute-start(bf16[1,384,768]{2,1,0:T(8,128)(2,1)S(1)} %slice.131), channel_id=1, source_target_pairs={{0,16},{4,20},{8,24},{12,28},{16,0},{20,4},{24,8},{28,12},{1,17},{... | collective-permute-start | bytes 1769480 | tf_op jit(solution)/shard_map/ppermute | solution.py:516
  456.1 37.9 %collective-permute-start.56 = (bf16[1,384,768]{2,1,0:T(8,128)(2,1)S(1)}, bf16[1,384,768]{2,1,0:T(8,128)(2,1)S(1)}, u32[]{:S(2)}, u32[]{:S(2)}) collective-permute-start(bf16[1,384,768]{2,1,0:T(8,128)(2,1)S(1)} %slice.135), channel_id=1, source_target_pairs={{0,16},{4,20},{8,24},{12,28},{16,0},{20,4},{24,8},{28,12},{1,17},{... | collective-permute-start | bytes 1769480 | tf_op jit(solution)/shard_map/ppermute | solution.py:516
  459.3 35.7 %collective-permute-start.47 = (bf16[1,768,384]{2,1,0:T(8,128)(2,1)S(1)}, bf16[1,768,384]{2,1,0:T(8,128)(2,1)S(1)}, u32[]{:S(2)}, u32[]{:S(2)}) collective-permute-start(bf16[1,768,384]{2,1,0:T(8,128)(2,1)S(1)} %slice.123), channel_id=1, source_target_pairs={{0,8},{4,12},{8,0},{12,4},{16,24},{20,28},{24,16},{28,20},{1,9},{5... | collective-permute-start | bytes 1769480 | tf_op jit(solution)/shard_map/ppermute | solution.py:516
  473.7 24.3 %collective-permute-start.50 = (bf16[1,768,384]{2,1,0:T(8,128)(2,1)}, bf16[1,768,384]{2,1,0:T(8,128)(2,1)}, u32[]{:S(2)}, u32[]{:S(2)}) collective-permute-start(bf16[1,768,384]{2,1,0:T(8,128)(2,1)} %slice.127), channel_id=1, source_target_pairs={{0,8},{4,12},{8,0},{12,4},{16,24},{20,28},{24,16},{28,20},{1,9},{5... | collective-permute-start | bytes 1769480 | tf_op jit(solution)/shard_map/ppermute | solution.py:516
  (70 other events, 944.4 us)
Sparse Core Ops, SparseCore 0:
  12.5 62.4 all-gather.1
  364.4 83.8 reduce-scatter.1
  495.4 39.5 all-reduce.2

commit v2 on v1

--- a/solution.py
+++ b/solution.py
@@ -19,6 +19,7 @@
 BF16 = jnp.bfloat16
 I32 = jnp.int32
 VMEM_LIMIT = 60 * 1024 * 1024
+MESH = pl.DeviceIdType.MESH
 
 
 def nn(left, right):
@@ -129,38 +130,12 @@
     return tail if last == 0 else jnp.concatenate([scores[:last], tail], axis=0)
 
 
-def forward_kernel(
-    experts,
-    local,
-    cap,
-    buckets,
-    shards,
-    here_ref,
-    tok_ref,
-    w_ref,
-    routes_ref,
-    routes_t_ref,
-    bucket_ref,
-    q_ref,
-    k_ref,
-    v_ref,
-    normed_ref,
-    merged_t_ref,
-    middle_ref,
-    second_ref,
-    gates_ref,
-    line_ref,
-    *rest,
-):
-    groups = experts // local
-    x_refs, slot_refs = rest[:experts], rest[experts : experts + groups]
-    v_t_ref, out_t_ref, twice_ref = rest[experts + groups :]
+def project_inputs(experts, buckets, shards, tok_ref, w_ref, bucket_ref, q_ref, k_ref, v_ref, normed_ref, v_t_ref, line_ref):
     n, width = tok_ref.shape
-    misc = w_ref[:, 4 * width :]
-    misc_t = jnp.transpose(misc.astype(F32))
-    gain_one, gain_two = misc_t[experts : experts + 1], misc_t[experts + 1 : experts + 2]
+    misc = w_ref[:, 3 * width : 3 * width + LANES]
+    gain = jnp.transpose(misc.astype(F32))[experts : experts + 1]
     x = tok_ref[...].astype(F32)
-    normed = x * lax.rsqrt(jnp.mean(x * x, axis=-1, keepdims=True) + EPSILON) * gain_one
+    normed = x * lax.rsqrt(jnp.mean(x * x, axis=-1, keepdims=True) + EPSILON) * gain
     normed_ref[...] = normed.astype(BF16)
     normed = normed_ref[...]
     q_ref[...] = (nn(normed, w_ref[:, :width]).astype(BF16).astype(F32) * SCALE).astype(BF16)
@@ -171,6 +146,10 @@
     table = table_rows(misc, buckets, shards).astype(BF16)
     by_bucket = hot(iota((buckets, n), 0) == bucket_ref[...])
     line_ref[...] = tn(table, by_bucket)[TABLE_AT : TABLE_AT + 16]
+
+
+def attend(q_ref, k_ref, v_t_ref, line_ref, twice_ref, merged_t_ref):
+    n = q_ref.shape[0]
     half = iota((1, LANES), 1) < HEAD_DIM
 
     def pair(hp, carry):
@@ -188,19 +167,22 @@
                 top = jnp.max(scores, axis=0, keepdims=True)
                 e = jnp.exp(scores - top)
                 probs = (e * (1.0 / jnp.sum(e, axis=0, keepdims=True))).astype(BF16)
-                out_t_ref[at, cols] = nn(v_t_ref[at, :rows], probs).astype(BF16)
+                merged_t_ref[at, cols] = nn(v_t_ref[at, :rows], probs).astype(BF16)
         return carry
 
     lax.fori_loop(0, HEADS // 2, pair, 0)
-    merged_t_ref[...] = out_t_ref[...]
-    middle = x + tn(merged_t_ref[...], w_ref[:, 3 * width : 4 * width])
+
+
+def route(experts, local, cap, here, tok_ref, w_ref, routes_ref, merged_t_ref, middle_ref, second_ref, gates_ref, slot_refs):
+    n, width = tok_ref.shape
+    misc = w_ref[:, 3 * width : 3 * width + LANES]
+    gain = jnp.transpose(misc.astype(F32))[experts + 1 : experts + 2]
+    middle = tok_ref[...].astype(F32) + tn(merged_t_ref[...], w_ref[:, 3 * width + LANES :])
     middle_ref[...] = middle
     second = middle * lax.rsqrt(jnp.mean(middle * middle, axis=-1, keepdims=True) + EPSILON)
-    second_ref[...] = (second * gain_two).astype(BF16)
-    second = second_ref[...]
-    here = here_ref[0]
+    second_ref[...] = (second * gain).astype(BF16)
     c0, c1, oh0, oh1 = places_by_row(routes_ref[...], here, local, cap)
-    logits = nn(second, misc)
+    logits = nn(second_ref[...], misc)
     p0 = jnp.sum(jnp.where(oh0, logits, 0.0), axis=1, keepdims=True)
     p1 = jnp.sum(jnp.where(oh1, logits, 0.0), axis=1, keepdims=True)
     top = jnp.maximum(p0, p1)
@@ -208,15 +190,197 @@
     g0, g1 = e0 / (e0 + e1), e1 / (e0 + e1)
     wide = iota((n, LANES), 1)
     gates_ref[...] = jnp.where(wide == 0, g0, jnp.where(wide == 1, g1, 0.0))
-    d0, d1 = places_by_lane(routes_t_ref[...], here, experts, local, cap)
-    for at, x_ref in enumerate(x_refs):
-        x_ref[...] = put_rows(second, d0, d1, at * cap, cap)
     for at, slot_ref in enumerate(slot_refs):
-        slot_ref[...] = jnp.zeros_like(slot_ref)
+        slot_ref[...] = jnp.zeros(slot_ref.shape, F32)
         for l in range(local):
             lane = iota((n, slot_ref.shape[1]), 1) + (at * local + l) * cap
             held = jnp.where(lane == c0, g0, jnp.where(lane == c1, g1, 0.0))
             slot_ref[l : l + 1, :] = jnp.sum(held, axis=0, keepdims=True)
+
+
+def forward_kernel(
+    experts, local, cap, buckets, shards,
+    here_ref, tok_ref, w_ref, routes_ref, routes_t_ref, bucket_ref,
+    q_ref, k_ref, v_ref, normed_ref, merged_t_ref, middle_ref, second_ref, gates_ref, line_ref,
+    *rest,
+):
+    groups = experts // local
+    x_refs, slot_refs = rest[:experts], rest[experts : experts + groups]
+    v_t_ref, twice_ref = rest[experts + groups :]
+    here = here_ref[0]
+    project_inputs(experts, buckets, shards, tok_ref, w_ref, bucket_ref, q_ref, k_ref, v_ref, normed_ref, v_t_ref, line_ref)
+    attend(q_ref, k_ref, v_t_ref, line_ref, twice_ref, merged_t_ref)
+    route(experts, local, cap, here, tok_ref, w_ref, routes_ref, merged_t_ref, middle_ref, second_ref, gates_ref, slot_refs)
+    d0, d1 = places_by_lane(routes_t_ref[...], here, experts, local, cap)
+    for at, x_ref in enumerate(x_refs):
+        x_ref[...] = put_rows(second_ref[...], d0, d1, at * cap, cap)
+
+
+def open_kernel(
+    experts, local, cap, buckets, shards,
+    tok_ref, wq_ref, wk_ref, wv_ref, wo_ref, small_ref, routes_ref, routes_t_ref, bucket_ref, cot_ref, up_ref, down_ref,
+    q_ref, k_ref, v_ref, normed_ref, merged_t_ref, middle_ref, second_ref, gates_ref, line_ref,
+    full_ref, up_a_ref, up_b_ref, down_a_ref, down_b_ref, x_in_ref, cot_in_ref, slots_in_ref,
+    w_ref, cot_out_ref, x_out_ref, slots_out_ref, v_t_ref, twice_ref,
+    w_send, w_recv, e_send, e_recv, z_send, z_recv, local_sem,
+):
+    groups = experts // local
+    me, here = lax.axis_index("dp"), lax.axis_index("expert")
+    n, width = tok_ref.shape
+    rows = wq_ref.shape[0]
+    across, along, core = me ^ 2, me ^ 4, me ^ 1
+    diagonal = me ^ 6
+    barrier = pltpu.get_barrier_semaphore()
+    for peer in (across, along, core):
+        pl.semaphore_signal(barrier, inc=1, device_id={"dp": peer}, device_id_type=MESH)
+    for m in range(1, groups):
+        pl.semaphore_signal(barrier, inc=1, device_id={"expert": here ^ m}, device_id_type=MESH)
+    pl.semaphore_wait(barrier, 3 + groups - 1)
+
+    def send(src, dst, sems, at, peer):
+        copy = pltpu.make_async_remote_copy(
+            src_ref=src, dst_ref=dst, send_sem=sems[0].at[at], recv_sem=sems[1].at[at],
+            device_id=peer, device_id_type=MESH,
+        )
+        copy.start()
+        return copy
+
+    first = 3 * width + LANES
+    parts = (slice(0, first), slice(first, first + width))
+    mine = pl.ds(pl.multiple_of(me * rows, 16), rows)
+    w_ref[mine, 0:width] = wq_ref[...]
+    w_ref[mine, width : 2 * width] = wk_ref[...]
+    w_ref[mine, 2 * width : 3 * width] = wv_ref[...]
+    w_ref[mine, 3 * width : first] = small_ref[...]
+    w_ref[mine, first:] = wo_ref[...]
+    w_sems = (w_send, w_recv)
+
+    def rows_of(owner, start=0, count=rows):
+        return pl.ds(pl.multiple_of(owner * rows + start, 16), count)
+
+    def w_copy(at, part, owner, peer, start=0, count=rows):
+        view = w_ref.at[rows_of(owner, start, count), parts[part]]
+        return send(view, view, w_sems, part * 8 + at, {"dp": peer})
+
+    def w_wait(at, part, owner, start=0, count=rows):
+        view = w_ref.at[rows_of(owner, start, count), parts[part]]
+        pltpu.make_async_remote_copy(
+            src_ref=view, dst_ref=view, send_sem=w_send.at[part * 8 + at], recv_sem=w_recv.at[part * 8 + at],
+            device_id={"dp": core}, device_id_type=MESH,
+        ).wait_recv()
+
+    w_copies = []
+    for part in range(2):
+        for at, peer in ((0, across), (1, along), (2, core)):
+            w_copies.append(w_copy(at, part, me, peer))
+
+    d0, d1 = places_by_lane(routes_t_ref[...], here, experts, local, cap)
+    z_sems = (z_send, z_recv)
+    z_copies, own_copies = [], []
+
+    def dispatch(values, out_ref, in_ref, base):
+        for l in range(local):
+            for m in [*range(1, groups), 0]:
+                out_ref[l, m] = put_rows(values, d0, d1, (m * local + l) * cap, cap)
+                if m:
+                    z_copies.append(
+                        send(out_ref.at[l, m], in_ref.at[l, m], z_sems, base + l * groups + m, {"expert": here ^ m})
+                    )
+                else:
+                    copy = pltpu.make_async_copy(out_ref.at[l, 0], in_ref.at[l, 0], local_sem.at[base + l * groups])
+                    copy.start()
+                    own_copies.append(copy)
+
+    dispatch(cot_ref[...], cot_out_ref, cot_in_ref, 0)
+    half = rows // 2
+    for part in range(2):
+        w_wait(0, part, across)
+        w_copies.append(w_copy(3, part, across, along, 0, half))
+        w_copies.append(w_copy(4, part, across, core))
+        w_wait(1, part, along)
+        w_copies.append(w_copy(5, part, along, across, half, half))
+        w_copies.append(w_copy(6, part, along, core))
+        if part == 0:
+            continue
+
+    e_sems = (e_send, e_recv)
+    e_copies = []
+    tables = ((up_ref, up_a_ref, up_b_ref), (down_ref, down_a_ref, down_b_ref))
+
+    def e_at(l, kind, step):
+        return (l * 2 + kind) * 7 + step
+
+    for l in range(local):
+        for kind, (own_ref, a_ref, b_ref) in enumerate(tables):
+            copy = pltpu.make_async_copy(own_ref.at[l], a_ref.at[l, 0], local_sem.at[2 * experts + l * 2 + kind])
+            copy.start()
+            own_copies.append(copy)
+            e_copies.append(send(own_ref.at[l], a_ref.at[l, 1], e_sems, e_at(l, kind, 0), {"dp": across}))
+            e_copies.append(send(own_ref.at[l], a_ref.at[l, 2], e_sems, e_at(l, kind, 1), {"dp": along}))
+            e_copies.append(send(own_ref.at[l], b_ref.at[l, 0], e_sems, e_at(l, kind, 3), {"dp": core}))
+
+    def w_finish(part):
+        w_wait(3, part, diagonal, 0, half)
+        w_wait(5, part, diagonal, half, half)
+        w_copies.append(w_copy(7, part, diagonal, core))
+        w_wait(2, part, core)
+        w_wait(4, part, core ^ 2)
+        w_wait(6, part, core ^ 4)
+        w_wait(7, part, core ^ 6)
+
+    w_finish(0)
+    project_inputs(experts, buckets, shards, tok_ref, w_ref, bucket_ref, q_ref, k_ref, v_ref, normed_ref, v_t_ref, line_ref)
+    attend(q_ref, k_ref, v_t_ref, line_ref, twice_ref, merged_t_ref)
+    w_finish(1)
+    copy = pltpu.make_async_copy(w_ref, full_ref, local_sem.at[2 * experts + 2 * local])
+    copy.start()
+    own_copies.append(copy)
+    route(
+        experts, local, cap, here, tok_ref, w_ref, routes_ref, merged_t_ref, middle_ref, second_ref, gates_ref,
+        [slots_out_ref.at[m] for m in range(groups)],
+    )
+    base = 2 * experts
+    for m in range(1, groups):
+        z_copies.append(send(slots_out_ref.at[m], slots_in_ref.at[m], z_sems, base + m, {"expert": here ^ m}))
+    copy = pltpu.make_async_copy(slots_out_ref.at[0], slots_in_ref.at[0], local_sem.at[2 * experts + 2 * local + 1])
+    copy.start()
+    own_copies.append(copy)
+    dispatch(second_ref[...], x_out_ref, x_in_ref, experts)
+
+    def e_wait(l, kind, step, slab_ref):
+        at = e_at(l, kind, step)
+        pltpu.make_async_remote_copy(
+            src_ref=slab_ref, dst_ref=slab_ref, send_sem=e_send.at[at], recv_sem=e_recv.at[at],
+            device_id={"dp": core}, device_id_type=MESH,
+        ).wait_recv()
+
+    for l in range(local):
+        for kind, (own_ref, a_ref, b_ref) in enumerate(tables):
+            step = kind
+            e_wait(l, kind, step, a_ref.at[l, 1 + step])
+            e_copies.append(
+                send(a_ref.at[l, 1 + step], a_ref.at[l, 3], e_sems, e_at(l, kind, 2), {"dp": along if kind == 0 else across})
+            )
+            e_copies.append(send(a_ref.at[l, 1 + step], b_ref.at[l, 1 + step], e_sems, e_at(l, kind, 4 + step), {"dp": core}))
+    for l in range(local):
+        for kind, (own_ref, a_ref, b_ref) in enumerate(tables):
+            step = 1 - kind
+            e_wait(l, kind, step, a_ref.at[l, 1 + step])
+            e_copies.append(send(a_ref.at[l, 1 + step], b_ref.at[l, 1 + step], e_sems, e_at(l, kind, 4 + step), {"dp": core}))
+    for l in range(local):
+        for kind, (own_ref, a_ref, b_ref) in enumerate(tables):
+            e_wait(l, kind, 2, a_ref.at[l, 3])
+            e_copies.append(send(a_ref.at[l, 3], b_ref.at[l, 3], e_sems, e_at(l, kind, 6), {"dp": core}))
+    for l in range(local):
+        for kind, (own_ref, a_ref, b_ref) in enumerate(tables):
+            for i in range(4):
+                e_wait(l, kind, 3 + i, b_ref.at[l, i])
+    for copy in z_copies:
+        copy.wait()
+    for copy in e_copies + w_copies:
+        copy.wait_send()
+    for copy in own_copies:
+        copy.wait()
 
 
 def gelu_both(v):
@@ -232,32 +396,29 @@
 
 def expert_kernel(local_at, groups, cap, *refs):
     take = iter(refs)
-    row_refs = [next(take) for _ in range(groups)]
-    cot_refs = [next(take) for _ in range(groups)]
-    slot_refs = [next(take) for _ in range(groups)]
-    up_a, up_b, down_a, down_b = (next(take) for _ in range(4))
+    rows_in, cots_in, slots_in, up_a, up_b, down_a, down_b = (next(take) for _ in range(7))
     reply_refs = [next(take) for _ in range(groups)]
     back_refs = [next(take) for _ in range(groups)]
     dot_refs = [next(take) for _ in range(groups)]
     ug_a, ug_b, dg_a, dg_b = (next(take) for _ in range(4))
     x_ref, xt_ref, cot_ref, gr_ref, reply_ref, back_ref = (next(take) for _ in range(6))
     up_buf, down_buf, ug_buf, dg_buf, act_ref, gh_ref = (next(take) for _ in range(6))
-    in_sem, out_sem = next(take), next(take)
+    in_sem, out_sem, row_sem = take
     rows, width = x_ref.shape
-    slab = up_a.shape[2]
+    slab = up_a.shape[3]
     block = up_buf.shape[2]
     per = block // slab
-    half = up_a.shape[0] // per
+    half = up_a.shape[1] // per
     steps = 2 * half
 
     def fetches(up, down, at, slot):
         for i in range(per):
             cut = slice(i * slab, (i + 1) * slab)
             yield pltpu.make_async_copy(
-                up.at[at * per + i], up_buf.at[slot, :, cut], in_sem.at[slot, i]
+                up.at[local_at, at * per + i], up_buf.at[slot, :, cut], in_sem.at[slot, i]
             )
             yield pltpu.make_async_copy(
-                down.at[at + i * half], down_buf.at[slot, cut, :], in_sem.at[slot, per + i]
+                down.at[local_at, at * per + i], down_buf.at[slot, cut, :], in_sem.at[slot, per + i]
             )
 
     def stores(up, down, at, slot):
@@ -267,7 +428,7 @@
                 ug_buf.at[slot, :, cut], up.at[at * per + i], out_sem.at[slot, i]
             )
             yield pltpu.make_async_copy(
-                dg_buf.at[slot, cut, :], down.at[at + i * half], out_sem.at[slot, per + i]
+                dg_buf.at[slot, cut, :], down.at[at * per + i], out_sem.at[slot, per + i]
             )
 
     def begin(kind, first, second, step, slot):
@@ -282,16 +443,20 @@
                 copy.start()
 
     begin(fetches, (up_a, down_a), (up_b, down_b), 0, 0)
+    copies = []
     for m in range(groups):
         cut = slice(m * cap, (m + 1) * cap)
-        x_ref[cut, :] = row_refs[m][...]
-        slots = jnp.broadcast_to(
-            slot_refs[m][local_at : local_at + 1, :], (LANES, slot_refs[m].shape[1])
-        )
-        gate = jnp.transpose(slots)[:cap, 0:1]
-        cot = cot_refs[m][...]
-        cot_ref[cut, :] = cot
-        gr_ref[cut, :] = (gate * cot.astype(F32)).astype(BF16)
+        copies.append(pltpu.make_async_copy(rows_in.at[local_at, m], x_ref.at[cut, :], row_sem.at[0, m]))
+        copies.append(pltpu.make_async_copy(cots_in.at[local_at, m], cot_ref.at[cut, :], row_sem.at[1, m]))
+    for copy in copies:
+        copy.start()
+    for copy in copies:
+        copy.wait()
+    for m in range(groups):
+        cut = slice(m * cap, (m + 1) * cap)
+        slots = slots_in[m, local_at : local_at + 1, :]
+        gate = jnp.transpose(jnp.broadcast_to(slots, (LANES, slots.shape[1])))[:cap, 0:1]
+        gr_ref[cut, :] = (gate * cot_ref[cut, :].astype(F32)).astype(BF16)
     xt_ref[...] = jnp.transpose(x_ref[...])
     reply_ref[...] = jnp.zeros_like(reply_ref)
     back_ref[...] = jnp.zeros_like(back_ref)
@@ -370,7 +535,7 @@
     inputs_grad_ref, grads_ref = next(take), next(take)
     gm_ref, gmid_ref, k_t_ref, gq_t_ref, gk_ref, gv_ref, fold_ref, twice_ref = take
     n, width = tok_ref.shape
-    misc = w_ref[:, 4 * width :]
+    misc = w_ref[:, 3 * width : 3 * width + LANES]
     misc_t = jnp.transpose(misc.astype(F32))
     gain_one, gain_two = misc_t[experts : experts + 1], misc_t[experts + 1 : experts + 2]
     c0, c1, oh0, oh1 = places_by_row(routes_ref[...], here_ref[0], local, cap)
@@ -398,8 +563,8 @@
     gmid = cot_ref[...].astype(F32) + r * (u - mr * jnp.mean(u * mr, axis=-1, keepdims=True))
     gmid_ref[...] = gmid
     branch = gmid.astype(BF16)
-    grads_ref[:, 3 * width : 4 * width] = nn(merged_t_ref[...], branch).astype(BF16)
-    gm_ref[...] = nt(branch, w_ref[:, 3 * width : 4 * width]).astype(BF16)
+    grads_ref[:, 3 * width + LANES :] = nn(merged_t_ref[...], branch).astype(BF16)
+    gm_ref[...] = nt(branch, w_ref[:, 3 * width + LANES :]).astype(BF16)
     k_t_ref[...] = jnp.transpose(k_ref[...])
     half = iota((1, LANES), 1) < HEAD_DIM
 
@@ -495,7 +660,7 @@
     tall = iota((LANES, width), 0)
     gains = jnp.where(tall == experts, prenorm_grad, jnp.where(tall == experts + 1, midnorm_grad, 0.0))
     small = router_grad + jnp.transpose(gains) + nn(select, table_grad)
-    grads_ref[:, 4 * width :] = small.astype(BF16)
+    grads_ref[:, 3 * width : 3 * width + LANES] = small.astype(BF16)
 
 
 def combine_kernel(local, cap, here_ref, routes_ref, gates_ref, middle_ref, *rest):
@@ -518,13 +683,6 @@
 
 def swap_all(values):
     return [v if m == 0 else swap(v, "expert", m) for m, v in enumerate(values)]
-
-
-def gather_slabs(slab, bits):
-    held = slab[None]
-    for bit in bits[:-1]:
-        held = jnp.concatenate([held, swap(held, "dp", bit)], axis=0)
-    return held, swap(held, "dp", bits[-1])
 
 
 def reduce_slabs(kept, sent, bits):
@@ -585,67 +743,85 @@
         ],
         axis=1,
     )
-    packed = jnp.concatenate(
-        [query_weight, key_weight, value_weight, project_weight, small], axis=1
-    )
-    full = lax.all_gather(packed, "dp", axis=0, tiled=True)
-
-    cot_out = vmem_call(
-        functools.partial(scatter_kernel, experts, local, cap),
-        "send_cotangent",
-        [shape((cap, width))] * experts,
-        specs=[smem, vmem, vmem],
-        flops=2 * n * experts * cap * width,
-        moved=4 * experts * cap * width,
-    )(here, routes_t, cotangent)
-    cot_in = [swap_all(cot_out[l::local]) for l in range(local)]
-
+    packed_width = 4 * width + LANES
+    slots_shape = (groups, 8, 256)
+    kept = [shape((n, width))] * 4 + [
+        shape((width, n)),
+        shape((n, width), F32),
+        shape((n, width)),
+        shape((n, LANES), F32),
+        shape((16, n), F32),
+    ]
     if direct:
-        ups = [gather_slabs(up_weight[l], (2, 4, 1)) for l in range(local)]
-        downs = [gather_slabs(down_weight[l], (4, 2, 1)) for l in range(local)]
+        slabs_up, slabs_down = shape((local, 4, width, slab)), shape((local, 4, slab, width))
+        moved_rows = shape((local, groups, cap, width))
+        outs = pl.pallas_call(
+            functools.partial(open_kernel, experts, local, cap, buckets, shards),
+            name="open",
+            out_shape=kept
+            + [shape((width, packed_width)), slabs_up, slabs_up, slabs_down, slabs_down]
+            + [moved_rows, moved_rows, shape(slots_shape, F32)],
+            in_specs=[vmem] * 10 + [hbm] * 2,
+            out_specs=[vmem] * 9 + [hbm] * 8,
+            scratch_shapes=[
+                pltpu.VMEM((width, packed_width), BF16),
+                pltpu.VMEM((local, groups, cap, width), BF16),
+                pltpu.VMEM((local, groups, cap, width), BF16),
+                pltpu.VMEM(slots_shape, F32),
+                pltpu.VMEM((width, n), BF16),
+                pltpu.VMEM((LANES, 2 * n), F32),
+                pltpu.SemaphoreType.DMA((16,)),
+                pltpu.SemaphoreType.DMA((16,)),
+                pltpu.SemaphoreType.DMA((14 * local,)),
+                pltpu.SemaphoreType.DMA((14 * local,)),
+                pltpu.SemaphoreType.DMA((2 * experts + groups,)),
+                pltpu.SemaphoreType.DMA((2 * experts + groups,)),
+                pltpu.SemaphoreType.DMA((2 * experts + 2 * local + 2,)),
+            ],
+            compiler_params=pltpu.CompilerParams(
+                vmem_limit_bytes=VMEM_LIMIT, collective_id=0, has_side_effects=True
+            ),
+            cost_estimate=pl.CostEstimate(flops=20 * 10**9, bytes_accessed=300 * 10**6, transcendentals=0),
+        )(
+            tokens, query_weight, key_weight, value_weight, project_weight, small,
+            routes, routes_t, bucket_row, cotangent, up_weight, down_weight,
+        )
+        q, k, v, normed, merged_t, middle, second, gates, line, full = outs[:10]
+        weights, (x_in, cot_in, slots_in) = outs[10:14], outs[14:]
     else:
+        packed = jnp.concatenate(
+            [query_weight, key_weight, value_weight, small, project_weight], axis=1
+        )
+        full = lax.all_gather(packed, "dp", axis=0, tiled=True)
+        cot_out = vmem_call(
+            functools.partial(scatter_kernel, experts, local, cap),
+            "send_cotangent",
+            [shape((cap, width))] * experts,
+            specs=[smem, vmem, vmem],
+        )(here, routes_t, cotangent)
         up_all = lax.all_gather(up_weight, "dp", axis=2, tiled=True)
         down_all = lax.all_gather(down_weight, "dp", axis=1, tiled=True)
-        ups, downs = [], []
-        for l in range(local):
-            u = up_all[l].reshape(width, hidden // width, width).transpose(1, 0, 2)
-            d = down_all[l].reshape(hidden // width, width, width)
-            cut = hidden // width // 2
-            ups.append((u[:cut], u[cut:]))
-            downs.append((d[:cut], d[cut:]))
-
-    forward = vmem_call(
-        functools.partial(forward_kernel, experts, local, cap, buckets, shards),
-        "attention_forward",
-        [shape((n, width))] * 4
-        + [
-            shape((width, n)),
-            shape((n, width), F32),
-            shape((n, width)),
-            shape((n, LANES), F32),
-            shape((16, n), F32),
-        ]
-        + [shape((cap, width))] * experts
-        + [shape((8, 256), F32)] * groups,
-        scratch=[
-            pltpu.VMEM((width, n), BF16),
-            pltpu.VMEM((width, n), BF16),
-            pltpu.VMEM((LANES, 2 * n), F32),
-        ],
-        specs=[smem] + [vmem] * 5,
-        flops=20 * 10**9,
-        moved=20 * 10**6,
-    )(here, tokens, full, routes, routes_t, bucket_row)
-    q, k, v, normed, merged_t, middle, second, gates, line = forward[:9]
-    x_out, slots_out = forward[9 : 9 + experts], forward[9 + experts :]
-    slots_in = swap_all(slots_out)
-    x_in = [swap_all(x_out[l::local]) for l in range(local)]
+        up_all = up_all.reshape(local, width, hidden // width, width).transpose(0, 2, 1, 3)
+        down_all = down_all.reshape(local, hidden // width, width, width)
+        cut = hidden // width // 2
+        weights = (up_all[:, :cut], up_all[:, cut:], down_all[:, :cut], down_all[:, cut:])
+        forward = vmem_call(
+            functools.partial(forward_kernel, experts, local, cap, buckets, shards),
+            "attention_forward",
+            kept + [shape((cap, width))] * experts + [shape((8, 256), F32)] * groups,
+            scratch=[pltpu.VMEM((width, n), BF16), pltpu.VMEM((LANES, 2 * n), F32)],
+            specs=[smem] + [vmem] * 5,
+        )(here, tokens, full, routes, routes_t, bucket_row)
+        q, k, v, normed, merged_t, middle, second, gates, line = forward[:9]
+        x_out, slots_out = forward[9 : 9 + experts], forward[9 + experts :]
+        slots_in = jnp.stack(swap_all(slots_out))
+        x_in = jnp.stack([jnp.stack(swap_all(x_out[l::local])) for l in range(local)])
+        cot_in = jnp.stack([jnp.stack(swap_all(cot_out[l::local])) for l in range(local)])
 
     rows = groups * cap
     replies, backs, dots, up_grads, down_grads = [], [], [], [], []
     for l in range(local):
-        up, down = ups[l], downs[l]
-        count, slab_width = up[0].shape[0], up[0].shape[2]
+        count, slab_width = weights[0].shape[1], weights[0].shape[3]
         per = width // slab_width
         outs = pl.pallas_call(
             functools.partial(expert_kernel, l, groups, cap),
@@ -654,7 +830,7 @@
             + [shape((8, 256), F32)] * groups
             + [shape((count, width, slab_width))] * 2
             + [shape((count, slab_width, width))] * 2,
-            in_specs=[vmem] * (3 * groups) + [hbm] * 4,
+            in_specs=[hbm, hbm, vmem] + [hbm] * 4,
             out_specs=[vmem] * (3 * groups) + [hbm] * 4,
             scratch_shapes=[
                 pltpu.VMEM((rows, width), BF16),
@@ -671,19 +847,20 @@
                 pltpu.VMEM((rows, width), BF16),
                 pltpu.SemaphoreType.DMA((2, 2 * per)),
                 pltpu.SemaphoreType.DMA((2, 2 * per)),
+                pltpu.SemaphoreType.DMA((2, groups)),
             ],
             compiler_params=pltpu.CompilerParams(vmem_limit_bytes=VMEM_LIMIT),
             cost_estimate=pl.CostEstimate(
                 flops=12 * rows * width * hidden, bytes_accessed=40 * 10**6, transcendentals=0
             ),
-        )(*x_in[l], *cot_in[l], *slots_in, *up, *down)
+        )(x_in, cot_in, slots_in, *weights)
         replies.append(outs[:groups])
         backs.append(swap_all(outs[groups : 2 * groups]))
         dots.append(swap_all(outs[2 * groups : 3 * groups]))
         ug, dg = outs[3 * groups : 3 * groups + 2], outs[3 * groups + 2 :]
         if direct:
             up_grads.append(reduce_slabs(*ug, (2, 4, 1)))
-            down_grads.append(reduce_slabs(*dg, (4, 2, 1)))
+            down_grads.append(reduce_slabs(*dg, (2, 4, 1)))
         else:
             ug = jnp.concatenate(ug, axis=0).transpose(1, 0, 2).reshape(width, hidden)
             dg = jnp.concatenate(dg, axis=0).reshape(hidden, width)
@@ -696,7 +873,7 @@
     inputs_grad, grads = vmem_call(
         functools.partial(backward_kernel, experts, local, cap, buckets, shards),
         "attention_backward",
-        [shape((n, width)), shape((width, packed.shape[1]))],
+        [shape((n, width)), shape((width, packed_width))],
         scratch=[
             pltpu.VMEM((n, width), BF16),
             pltpu.VMEM((n, width), F32),
@@ -742,14 +919,14 @@
         moved=6 * 10**6,
     )(here, routes, gates, middle, *replies)
 
-    at = 4 * width
+    at = 3 * width
     return (
         layer_out,
         inputs_grad,
         totals[:, :width],
         totals[:, width : 2 * width],
         totals[:, 2 * width : 3 * width],
-        totals[:, 3 * width : at],
+        totals[:, at + LANES :],
         totals[:, at : at + experts],
         totals[:, at + experts],
         totals[:, at + experts + 1],

time: 548 us -> 480 us (0.88); the launches traced: 547 us -> 472 us
  Pallas kernels: 143 us -> 221 us
  waiting for transfers between devices: 237 us -> 160 us
  starting transfers between devices: 97.4 us -> 40.7 us
  other arithmetic: 33.9 us -> 17.1 us
    pallas_call x0 -> x1, Pallas kernels: none -> 111 us  [body(): pl.pallas_call(functools.partial(open_kernel, experts, local, cap, bucket...]
    ppermute x57 -> x30, waiting for transfers between devices: 203 us -> 136 us  [swap(): lax.ppermute(value, axis, [(i, i ^ bit) for i in range(lax.axis_size(axis...]
    ppermute x57 -> x30, starting transfers between devices: 97.2 us -> 40.6 us  [swap(): lax.ppermute(value, axis, [(i, i ^ bit) for i in range(lax.axis_size(axis...]
    pallas_call x4 -> x2, Pallas kernels: 75.9 us -> 41.4 us  [call(): pl.pallas_call(body, name=name, out_shape=out_shape, in_specs=in_specs, o...]
    concatenate x8 -> x0, other arithmetic: 16.8 us -> none  [gather_slabs(): held = jnp.concatenate([held, swap(held, 'dp', bit)], axis=0)]
    psum x1, waiting for transfers between devices: 34.2 us -> 24.3 us  [body(): totals = lax.psum(shares, 'expert').astype(F32)]
  transfers between devices with their start and end apart: 60 -> 32, of which waited for: 25 -> 13; matrix products, arithmetic and copies ran while one was open for 7% -> 5% of each run, Pallas kernels for 18% -> 9%
where the time goes in v2:
time: 480 us; the launch traced here: 472 us
  Pallas kernels  221 us (46%)
  waiting for transfers between devices  160 us (33%)
  starting transfers between devices  40.7 us (8%)
  local copies, waits for them, and re-layouts  18.3 us (4%)
  other arithmetic  17.1 us (4%)
  between operations  14.7 us (3%)
    ppermute x30, waiting for transfers between devices, swap(): lax.ppermute(value, axis, [(i, i ^ bit) for i in range(lax.axis_size(axis...  136 us
    pallas_call x1, Pallas kernels, body(): pl.pallas_call(functools.partial(open_kernel, experts, local, cap, bucket...  111 us
    pallas_call x2, Pallas kernels, body(): pl.pallas_call(functools.partial(expert_kernel, l, groups, cap), name='ex...  68.3 us
    pallas_call x2, Pallas kernels, call(): pl.pallas_call(body, name=name, out_shape=out_shape, in_specs=in_specs, o...  41.4 us
    ppermute x30, starting transfers between devices, swap(): lax.ppermute(value, axis, [(i, i ^ bit) for i in range(lax.axis_size(axis...  40.6 us
    psum x1, waiting for transfers between devices, body(): totals = lax.psum(shares, 'expert').astype(F32)  24.3 us
  transfers between devices with their start and end apart: 32, of which 13 were waited for; matrix products, arithmetic and copies ran while one was open for 5% of the time, Pallas kernels for 9%

profile of v2, /device:TPU:0, one launch (start us, length us, event | category | flops | bytes accessed | tf_op | source)
XLA Modules:
  0.0 471.8 jit_solution(6867795848390524013)
XLA Ops:
  7.2 1.5 copy.37.routes_ref
  12.5 111.3 %open.1 = (bf16[512,768]{1,0:T(8,128)(2,1)}, bf16[512,768]{1,0:T(8,128)(2,1)}, bf16[512,768]{1,0:T(8,128)(2,1)}, bf16[512,768]{1,0:T(8,128)(2,1)}, bf16[768,512]...) custom-call(bf16[512,768]{1,0:T(8,128)(2,1)} %tok_ref.3, ...), custom_call_target="tpu_custom_call" | custom-call | flops 20000000000 | bytes 300000000 | tf_op jit(solution)/shard_map/open/pallas_call | solution.py:758
  123.8 34.3 %expert.3 = (bf16[192,768]{1,0:T(8,128)(2,1)}, bf16[192,768]{1,0:T(8,128)(2,1)}, bf16[192,768]{1,0:T(8,128)(2,1)}, bf16[192,768]{1,0:T(8,128)(2,1)}, bf16[192,76...) custom-call(bf16[2,4,192,768]{3,2,1,0:T(8,128)(2,1)} %get-tuple-elem, ...), custom_call_target="tpu_custom_call" | custom-call | flops 21743271936 | bytes 40000000 | tf_op jit(solution)/shard_map/expert/pallas_call | solution.py:826
  158.1 1.6 collective-permute-start.11
  159.7 3.9 collective-permute-start.13
  163.6 2.4 collective-permute-start.17
  165.9 34.1 %expert.2 = (bf16[192,768]{1,0:T(8,128)(2,1)}, bf16[192,768]{1,0:T(8,128)(2,1)}, bf16[192,768]{1,0:T(8,128)(2,1)}, bf16[192,768]{1,0:T(8,128)(2,1)}, bf16[192,76...) custom-call(bf16[2,4,192,768]{3,2,1,0:T(8,128)(2,1)} %get-tuple-elem, ...), custom_call_target="tpu_custom_call" | custom-call | flops 21743271936 | bytes 40000000 | tf_op jit(solution)/shard_map/expert/pallas_call | solution.py:826
  200.0 1.2 collective-permute-start.12
  202.1 2.4 collective-permute-start.16
  204.8 1.9 collective-permute-start.9
  206.7 2.4 collective-permute-start.10
  209.1 2.0 collective-permute-start.8
  211.1 8.0 %collective-permute-done.7.rest_3_ = bf16[192,768]{1,0:T(8,128)(2,1)S(1)} collective-permute-done((bf16[192,768]{1,0:T(8,128)(2,1)S(1)}, bf16[192,768]{1,0:T(8,128)(2,1)S(1)}, u32[]{:S(2)}, u32[]{:S(2)}) %collective-permute-start.7) | collective-permute-done | bytes 294944 | tf_op jit(solution)/shard_map/ppermute | solution.py:681
  219.1 9.3 %collective-permute-done.9.rest_5_ = bf16[192,768]{1,0:T(8,128)(2,1)S(1)} collective-permute-done((bf16[192,768]{1,0:T(8,128)(2,1)S(1)}, bf16[192,768]{1,0:T(8,128)(2,1)S(1)}, u32[]{:S(2)}, u32[]{:S(2)}) %collective-permute-start.9) | collective-permute-done | bytes 294944 | tf_op jit(solution)/shard_map/ppermute | solution.py:681
  228.4 3.0 collective-permute-done.6.rest_2_
  231.3 12.4 %collective-permute-done.8.rest_4_ = bf16[192,768]{1,0:T(8,128)(2,1)S(1)} collective-permute-done((bf16[192,768]{1,0:T(8,128)(2,1)}, bf16[192,768]{1,0:T(8,128)(2,1)S(1)}, u32[]{:S(2)}, u32[]{:S(2)}) %collective-permute-start.8) | collective-permute-done | bytes 294944 | tf_op jit(solution)/shard_map/ppermute | solution.py:681
  244.5 34.1 %attention_backward.1 = (bf16[512,768]{1,0:T(8,128)(2,1)}, bf16[768,3200]{1,0:T(8,128)(2,1)}) custom-call(s32[1]{0:T(128)} %bitcast.here_ref, bf16[512,768]{1,0:T(8,128)(2,1)} %tok_ref.3, bf16[768,3200]{1,0:T(8,128)(2,1)} %get-tuple-element.80.w_ref, s32[512,2]{1,0:T(8,128)} %copy.37.routes_ref, s32[1,512]{1,0:T(1,128)} %bitcast.9, ...), custom_call_target="tpu_custom_call" | custom-call | flops 40000000000 | bytes 30000000 | tf_op jit(solution)/shard_map/attention_backward/pallas_call | solution.py:48
  278.7 1.6 copy-done.10
  281.3 6.8 %collective-permute-done.24 = bf16[4,384,768]{2,1,0:T(8,128)(2,1)S(1)} collective-permute-done((bf16[4,384,768]{2,1,0:T(8,128)(2,1)S(1)}, bf16[4,384,768]{2,1,0:T(8,128)(2,1)S(1)}, u32[]{:S(2)}, u32[]{:S(2)}) %collective-permute-start.24) | collective-permute-done | bytes 2359328 | tf_op jit(solution)/shard_map/ppermute | solution.py:681
  288.1 2.2 add_convert_fusion.1
  291.5 1.5 collective-permute-start.25
  294.7 1.5 collective-permute-start.5
  296.2 13.6 %collective-permute-done.3.rest_5_ = bf16[192,768]{1,0:T(8,128)(2,1)S(1)} collective-permute-done((bf16[192,768]{1,0:T(8,128)(2,1)S(1)}, bf16[192,768]{1,0:T(8,128)(2,1)S(1)}, u32[]{:S(2)}, u32[]{:S(2)}) %collective-permute-start.3) | collective-permute-done | bytes 294944 | tf_op jit(solution)/shard_map/ppermute | solution.py:681
  309.8 1.4 collective-permute-start.28
  313.0 4.3 collective-permute-start.2
  317.3 2.8 collective-permute-done.rest_2_
  320.1 2.7 collective-permute-start.4
  322.8 1.7 collective-permute-start.19
  325.1 1.2 slice.109
  326.9 10.9 %collective-permute-done.2.rest_4_ = bf16[192,768]{1,0:T(8,128)(2,1)S(1)} collective-permute-done((bf16[192,768]{1,0:T(8,128)(2,1)S(1)}, bf16[192,768]{1,0:T(8,128)(2,1)S(1)}, u32[]{:S(2)}, u32[]{:S(2)}) %collective-permute-start.2) | collective-permute-done | bytes 294944 | tf_op jit(solution)/shard_map/ppermute | solution.py:681
  337.8 1.5 collective-permute-start.22
  340.0 7.3 %layer_out.1 = bf16[512,768]{1,0:T(8,128)(2,1)} custom-call(s32[1]{0:T(128)} %bitcast.here_ref, s32[512,2]{1,0:T(8,128)} %copy.37.routes_ref, f32[512,128]{1,0:T(8,128)} %get-tuple-element.63.gates_ref, f32[512,768]{1,0:T(8,128)} %get-tuple-element.64.middle_ref, bf16[192,768]{1,0:T(8,128)(2,1)} %get-tuple-element.72.rest_0_, ...), custom_call_target="tpu_custom_call" | custom-call | flops 2415919104 | bytes 6000000 | tf_op jit(solution)/shard_map/layer_out/pallas_call | solution.py:48
  347.7 1.6 collective-permute-start.26
  349.2 16.4 %collective-permute-done.28 = bf16[2,384,768]{2,1,0:T(8,128)(2,1)} collective-permute-done((bf16[2,384,768]{2,1,0:T(8,128)(2,1)}, bf16[2,384,768]{2,1,0:T(8,128)(2,1)}, u32[]{:S(2)}, u32[]{:S(2)}) %collective-permute-start.28) | collective-permute-done | bytes 1179680 | tf_op jit(solution)/shard_map/ppermute | solution.py:681
  365.6 1.6 add_convert_fusion.4
  367.3 1.5 collective-permute-start.29
  368.8 22.1 %collective-permute-done.19 = bf16[2,768,384]{2,1,0:T(8,128)(2,1)} collective-permute-done((bf16[2,768,384]{2,1,0:T(8,128)(2,1)}, bf16[2,768,384]{2,1,0:T(8,128)(2,1)}, u32[]{:S(2)}, u32[]{:S(2)}) %collective-permute-start.19) | collective-permute-done | bytes 1179680 | tf_op jit(solution)/shard_map/ppermute | solution.py:681
  390.9 1.6 add_convert_fusion.7
  392.6 1.5 collective-permute-start.20
  394.1 21.3 %collective-permute-done.22 = bf16[2,768,384]{2,1,0:T(8,128)(2,1)} collective-permute-done((bf16[2,768,384]{2,1,0:T(8,128)(2,1)}, bf16[2,768,384]{2,1,0:T(8,128)(2,1)}, u32[]{:S(2)}, u32[]{:S(2)}) %collective-permute-start.22) | collective-permute-done | bytes 1179680 | tf_op jit(solution)/shard_map/ppermute | solution.py:681
  415.4 1.6 add_convert_fusion.6
  417.8 1.5 collective-permute-start.23
  420.8 2.8 pad_maximum_fusion.1
  423.6 9.1 %collective-permute-done.23 = bf16[1,768,384]{2,1,0:T(8,128)(2,1)} collective-permute-done((bf16[1,768,384]{2,1,0:T(8,128)(2,1)}, bf16[1,768,384]{2,1,0:T(8,128)(2,1)}, u32[]{:S(2)}, u32[]{:S(2)}) %collective-permute-start.23) | collective-permute-done | bytes 589856 | tf_op jit(solution)/shard_map/ppermute | solution.py:681
  432.7 1.2 convert_add_fusion.2
  433.9 1.6 pad_maximum_fusion
  435.4 24.3 %all-reduce.3.cloned.1.call-done = bf16[96,3200]{1,0:T(8,128)(2,1)} async-done(((bf16[96,3200]{1,0:T(8,128)(2,1)}), bf16[96,3200]{1,0:T(8,128)(2,1)}) %all-reduce.3.cloned.1.call-update) | async-done | bytes 614416 | tf_op jit(solution)/shard_map/psum | solution.py:910
  459.8 1.2 convert_element_type.101
  (133 shorter events, 19.7 us)
Async XLA Ops:
  7.2 413.6 %reduce-scatter.2.cloned.1.call-start = ((), (), s32[]{:S(2)}) async-start(), calls=%async_computation.1 | async-start | bytes 5529600 | tf_op jit(solution)/shard_map/reduce_scatter | solution.py:909
  158.1 50.9 %collective-permute-start.11 = (bf16[192,768]{1,0:T(8,128)(2,1)}, bf16[192,768]{1,0:T(8,128)(2,1)S(1)}, u32[]{:S(2)}, u32[]{:S(2)}) collective-permute-start(bf16[192,768]{1,0:T(8,128)(2,1)} %get-tuple-element.95), channel_id=1, source_target_pairs={{0,3},{1,2},{2,1},{3,0},{4,7},{5,6},{6,5},{7,4},{8,11},{9,10},{10,... | collective-permute-start | bytes 884744 | tf_op jit(solution)/shard_map/ppermute | solution.py:681
  159.7 41.5 %collective-permute-start.13 = (f32[8,256]{1,0:T(8,128)}, f32[8,256]{1,0:T(8,128)S(1)}, u32[]{:S(2)}, u32[]{:S(2)}) collective-permute-start(f32[8,256]{1,0:T(8,128)} %get-tuple-element.99), channel_id=1, source_target_pairs={{0,1},{1,0},{2,3},{3,2},{4,5},{5,4},{6,7},{7,6},{8,9},{9,8},{10,11... | collective-permute-start | bytes 24584 | tf_op jit(solution)/shard_map/ppermute | solution.py:681
  163.6 38.6 %collective-permute-start.15 = (f32[8,256]{1,0:T(8,128)}, f32[8,256]{1,0:T(8,128)S(1)}, u32[]{:S(2)}, u32[]{:S(2)}) collective-permute-start(f32[8,256]{1,0:T(8,128)} %get-tuple-element.101), channel_id=1, source_target_pairs={{0,2},{1,3},{2,0},{3,1},{4,6},{5,7},{6,4},{7,5},{8,10},{9,11},{10,... | collective-permute-start | bytes 24584 | tf_op jit(solution)/shard_map/ppermute | solution.py:681
  163.6 40.9 %copy-start.19 = (bf16[192,768]{1,0:T(8,128)(2,1)S(1)}, bf16[192,768]{1,0:T(8,128)(2,1)}, u32[]{:S(2)}) copy-start(bf16[192,768]{1,0:T(8,128)(2,1)} %get-tuple-element.91) | copy-start | bytes 884740
  163.6 41.2 %copy-start.18 = (bf16[192,768]{1,0:T(8,128)(2,1)S(1)}, bf16[192,768]{1,0:T(8,128)(2,1)}, u32[]{:S(2)}) copy-start(bf16[192,768]{1,0:T(8,128)(2,1)} %get-tuple-element.93) | copy-start | bytes 884740
  163.6 40.9 %collective-permute-start.17 = (f32[8,256]{1,0:T(8,128)}, f32[8,256]{1,0:T(8,128)S(1)}, u32[]{:S(2)}, u32[]{:S(2)}) collective-permute-start(f32[8,256]{1,0:T(8,128)} %get-tuple-element.103), channel_id=1, source_target_pairs={{0,3},{1,2},{2,1},{3,0},{4,7},{5,6},{6,5},{7,4},{8,11},{9,10},{10,... | collective-permute-start | bytes 24584 | tf_op jit(solution)/shard_map/ppermute | solution.py:681
  200.0 4.8 %collective-permute-start.12 = (f32[8,256]{1,0:T(8,128)}, f32[8,256]{1,0:T(8,128)S(1)}, u32[]{:S(2)}, u32[]{:S(2)}) collective-permute-start(f32[8,256]{1,0:T(8,128)} %get-tuple-element.98), channel_id=1, source_target_pairs={{0,1},{1,0},{2,3},{3,2},{4,5},{5,4},{6,7},{7,6},{8,9},{9,8},{10,11... | collective-permute-start | bytes 24584 | tf_op jit(solution)/shard_map/ppermute | solution.py:681
  201.2 42.5 %copy-start.31 = (f32[8,256]{1,0:T(8,128)}, f32[8,256]{1,0:T(8,128)S(1)}, u32[]{:S(2)}) copy-start(f32[8,256]{1,0:T(8,128)S(1)} %collective-permute-done.13.rest_11_) | copy-start | bytes 24580
  201.2 5.4 %collective-permute-start.14 = (f32[8,256]{1,0:T(8,128)}, f32[8,256]{1,0:T(8,128)S(1)}, u32[]{:S(2)}, u32[]{:S(2)}) collective-permute-start(f32[8,256]{1,0:T(8,128)} %get-tuple-element.100), channel_id=1, source_target_pairs={{0,2},{1,3},{2,0},{3,1},{4,6},{5,7},{6,4},{7,5},{8,10},{9,11},{10,... | collective-permute-start | bytes 24584 | tf_op jit(solution)/shard_map/ppermute | solution.py:681
  202.1 41.6 %copy-start.32 = (f32[8,256]{1,0:T(8,128)}, f32[8,256]{1,0:T(8,128)S(1)}, u32[]{:S(2)}) copy-start(f32[8,256]{1,0:T(8,128)S(1)} %collective-permute-done.15.rest_13_) | copy-start | bytes 24580
  202.1 6.9 %collective-permute-start.16 = (f32[8,256]{1,0:T(8,128)}, f32[8,256]{1,0:T(8,128)S(1)}, u32[]{:S(2)}, u32[]{:S(2)}) collective-permute-start(f32[8,256]{1,0:T(8,128)} %get-tuple-element.102), channel_id=1, source_target_pairs={{0,3},{1,2},{2,1},{3,0},{4,7},{5,6},{6,5},{7,4},{8,11},{9,10},{10,... | collective-permute-start | bytes 24584 | tf_op jit(solution)/shard_map/ppermute | solution.py:681
  204.5 39.3 %copy-start.33 = (f32[8,256]{1,0:T(8,128)}, f32[8,256]{1,0:T(8,128)S(1)}, u32[]{:S(2)}) copy-start(f32[8,256]{1,0:T(8,128)S(1)} %collective-permute-done.17.rest_15_) | copy-start | bytes 24580
  204.5 14.6 %collective-permute-start.7 = (bf16[192,768]{1,0:T(8,128)(2,1)S(1)}, bf16[192,768]{1,0:T(8,128)(2,1)S(1)}, u32[]{:S(2)}, u32[]{:S(2)}) collective-permute-start(bf16[192,768]{1,0:T(8,128)(2,1)S(1)} %copy-done.19), channel_id=1, source_target_pairs={{0,1},{1,0},{2,3},{3,2},{4,5},{5,4},{6,7},{7,6},{8,9},{9,8},{10,11... | collective-permute-start | bytes 884744 | tf_op jit(solution)/shard_map/ppermute | solution.py:681
  204.8 39.0 %copy-start.34 = (f32[8,256]{1,0:T(8,128)}, f32[8,256]{1,0:T(8,128)S(1)}, u32[]{:S(2)}) copy-start(f32[8,256]{1,0:T(8,128)S(1)} %collective-permute-done.12.rest_10_) | copy-start | bytes 24580
  204.8 23.6 %collective-permute-start.9 = (bf16[192,768]{1,0:T(8,128)(2,1)S(1)}, bf16[192,768]{1,0:T(8,128)(2,1)S(1)}, u32[]{:S(2)}, u32[]{:S(2)}) collective-permute-start(bf16[192,768]{1,0:T(8,128)(2,1)S(1)} %copy-done.18), channel_id=1, source_target_pairs={{0,2},{1,3},{2,0},{3,1},{4,6},{5,7},{6,4},{7,5},{8,10},{9,11},{10,... | collective-permute-start | bytes 884744 | tf_op jit(solution)/shard_map/ppermute | solution.py:681
  206.7 37.1 %copy-start.35 = (f32[8,256]{1,0:T(8,128)}, f32[8,256]{1,0:T(8,128)S(1)}, u32[]{:S(2)}) copy-start(f32[8,256]{1,0:T(8,128)S(1)} %collective-permute-done.14.rest_12_) | copy-start | bytes 24580
  206.7 21.7 %collective-permute-start.10 = (bf16[192,768]{1,0:T(8,128)(2,1)}, bf16[192,768]{1,0:T(8,128)(2,1)S(1)}, u32[]{:S(2)}, u32[]{:S(2)}) collective-permute-start(bf16[192,768]{1,0:T(8,128)(2,1)} %get-tuple-element.94), channel_id=1, source_target_pairs={{0,3},{1,2},{2,1},{3,0},{4,7},{5,6},{6,5},{7,4},{8,11},{9,10},{10,... | collective-permute-start | bytes 884744 | tf_op jit(solution)/shard_map/ppermute | solution.py:681
  209.0 34.8 %copy-start.36 = (f32[8,256]{1,0:T(8,128)}, f32[8,256]{1,0:T(8,128)S(1)}, u32[]{:S(2)}) copy-start(f32[8,256]{1,0:T(8,128)S(1)} %collective-permute-done.16.rest_14_) | copy-start | bytes 24580
  209.0 22.3 %collective-permute-start.6 = (bf16[192,768]{1,0:T(8,128)(2,1)}, bf16[192,768]{1,0:T(8,128)(2,1)S(1)}, u32[]{:S(2)}, u32[]{:S(2)}) collective-permute-start(bf16[192,768]{1,0:T(8,128)(2,1)} %get-tuple-element.90), channel_id=1, source_target_pairs={{0,1},{1,0},{2,3},{3,2},{4,5},{5,4},{6,7},{7,6},{8,9},{9,8},{10,11... | collective-permute-start | bytes 884744 | tf_op jit(solution)/shard_map/ppermute | solution.py:681
  209.0 34.8 %copy-start.17 = (bf16[192,768]{1,0:T(8,128)(2,1)}, bf16[192,768]{1,0:T(8,128)(2,1)S(1)}, u32[]{:S(2)}) copy-start(bf16[192,768]{1,0:T(8,128)(2,1)S(1)} %collective-permute-done.11.rest_7_) | copy-start | bytes 884740
  209.1 34.7 %collective-permute-start.8 = (bf16[192,768]{1,0:T(8,128)(2,1)}, bf16[192,768]{1,0:T(8,128)(2,1)S(1)}, u32[]{:S(2)}, u32[]{:S(2)}) collective-permute-start(bf16[192,768]{1,0:T(8,128)(2,1)} %get-tuple-element.92), channel_id=1, source_target_pairs={{0,2},{1,3},{2,0},{3,1},{4,6},{5,7},{6,4},{7,5},{8,10},{9,11},{10,... | collective-permute-start | bytes 884744 | tf_op jit(solution)/shard_map/ppermute | solution.py:681
  219.1 24.7 %copy-start.22 = (bf16[192,768]{1,0:T(8,128)(2,1)}, bf16[192,768]{1,0:T(8,128)(2,1)S(1)}, u32[]{:S(2)}) copy-start(bf16[192,768]{1,0:T(8,128)(2,1)S(1)} %collective-permute-done.7.rest_3_) | copy-start | bytes 884740
  278.6 181.1 %all-reduce.3.cloned.1.call-start = ((), (), s32[]{:S(2)}) async-start(), calls=%async_computation.2 | async-start | bytes 1228800 | tf_op jit(solution)/shard_map/psum | solution.py:910
  280.3 7.9 %collective-permute-start.24 = (bf16[4,384,768]{2,1,0:T(8,128)(2,1)S(1)}, bf16[4,384,768]{2,1,0:T(8,128)(2,1)S(1)}, u32[]{:S(2)}, u32[]{:S(2)}) collective-permute-start(bf16[4,384,768]{2,1,0:T(8,128)(2,1)S(1)} %copy-done.10), channel_id=1, source_target_pairs={{0,4},{4,0},{8,12},{12,8},{16,20},{20,16},{24,28},{28,24},{1,5},{5... | collective-permute-start | bytes 7077896 | tf_op jit(solution)/shard_map/ppermute | solution.py:681
  280.3 11.2 %collective-permute-start.27 = (bf16[4,384,768]{2,1,0:T(8,128)(2,1)}, bf16[4,384,768]{2,1,0:T(8,128)(2,1)S(1)}, u32[]{:S(2)}, u32[]{:S(2)}) collective-permute-start(bf16[4,384,768]{2,1,0:T(8,128)(2,1)} %get-tuple-element.113), channel_id=1, source_target_pairs={{0,4},{4,0},{8,12},{12,8},{16,20},{20,16},{24,28},{28,24},{1,5},{5... | collective-permute-start | bytes 7077896 | tf_op jit(solution)/shard_map/ppermute | solution.py:681
  280.8 29.0 %collective-permute-start.18 = (bf16[4,768,384]{2,1,0:T(8,128)(2,1)}, bf16[4,768,384]{2,1,0:T(8,128)(2,1)S(1)}, u32[]{:S(2)}, u32[]{:S(2)}) collective-permute-start(bf16[4,768,384]{2,1,0:T(8,128)(2,1)} %get-tuple-element.107), channel_id=1, source_target_pairs={{0,4},{4,0},{8,12},{12,8},{16,20},{20,16},{24,28},{28,24},{1,5},{5... | collective-permute-start | bytes 7077896 | tf_op jit(solution)/shard_map/ppermute | solution.py:681
  280.8 42.1 %collective-permute-start.21 = (bf16[4,768,384]{2,1,0:T(8,128)(2,1)}, bf16[4,768,384]{2,1,0:T(8,128)(2,1)S(1)}, u32[]{:S(2)}, u32[]{:S(2)}) collective-permute-start(bf16[4,768,384]{2,1,0:T(8,128)(2,1)} %get-tuple-element.109), channel_id=1, source_target_pairs={{0,4},{4,0},{8,12},{12,8},{16,20},{20,16},{24,28},{28,24},{1,5},{5... | collective-permute-start | bytes 7077896 | tf_op jit(solution)/shard_map/ppermute | solution.py:681
  281.3 13.4 %collective-permute-start.1 = (bf16[192,768]{1,0:T(8,128)(2,1)S(1)}, bf16[192,768]{1,0:T(8,128)(2,1)S(1)}, u32[]{:S(2)}, u32[]{:S(2)}) collective-permute-start(bf16[192,768]{1,0:T(8,128)(2,1)S(1)} %copy-done.16), channel_id=1, source_target_pairs={{0,1},{1,0},{2,3},{3,2},{4,5},{5,4},{6,7},{7,6},{8,9},{9,8},{10,11... | collective-permute-start | bytes 884744 | tf_op jit(solution)/shard_map/ppermute | solution.py:681
  288.1 21.7 %collective-permute-start.3 = (bf16[192,768]{1,0:T(8,128)(2,1)S(1)}, bf16[192,768]{1,0:T(8,128)(2,1)S(1)}, u32[]{:S(2)}, u32[]{:S(2)}) collective-permute-start(bf16[192,768]{1,0:T(8,128)(2,1)S(1)} %copy-done.14), channel_id=1, source_target_pairs={{0,2},{1,3},{2,0},{3,1},{4,6},{5,7},{6,4},{7,5},{8,10},{9,11},{10,... | collective-permute-start | bytes 884744 | tf_op jit(solution)/shard_map/ppermute | solution.py:681
  291.5 55.8 %collective-permute-start.25 = (bf16[2,384,768]{2,1,0:T(8,128)(2,1)}, bf16[2,384,768]{2,1,0:T(8,128)(2,1)S(1)}, u32[]{:S(2)}, u32[]{:S(2)}) collective-permute-start(bf16[2,384,768]{2,1,0:T(8,128)(2,1)} %slice.113), channel_id=1, source_target_pairs={{0,16},{4,20},{8,24},{12,28},{16,0},{20,4},{24,8},{28,12},{1,17},{... | collective-permute-start | bytes 3538952 | tf_op jit(solution)/shard_map/ppermute | solution.py:681
  293.0 16.8 %copy-start.15 = (bf16[192,768]{1,0:T(8,128)(2,1)S(1)}, bf16[192,768]{1,0:T(8,128)(2,1)}, u32[]{:S(2)}) copy-start(bf16[192,768]{1,0:T(8,128)(2,1)} %get-tuple-element.74) | copy-start | bytes 884740
  293.5 18.3 %copy-start = (bf16[4,384,768]{2,1,0:T(8,128)(2,1)}, bf16[4,384,768]{2,1,0:T(8,128)(2,1)S(1)}, u32[]{:S(2)}) copy-start(bf16[4,384,768]{2,1,0:T(8,128)(2,1)S(1)} %add_convert_fusion) | copy-start | bytes 7077892
  293.5 17.7 %copy-start.9 = (bf16[4,768,384]{2,1,0:T(8,128)(2,1)S(1)}, bf16[4,768,384]{2,1,0:T(8,128)(2,1)}, u32[]{:S(2)}) copy-start(bf16[4,768,384]{2,1,0:T(8,128)(2,1)} %get-tuple-element.106) | copy-start | bytes 7077892
  294.7 18.3 %collective-permute-start.5 = (bf16[192,768]{1,0:T(8,128)(2,1)S(1)}, bf16[192,768]{1,0:T(8,128)(2,1)S(1)}, u32[]{:S(2)}, u32[]{:S(2)}) collective-permute-start(bf16[192,768]{1,0:T(8,128)(2,1)S(1)} %copy-done.12), channel_id=1, source_target_pairs={{0,3},{1,2},{2,1},{3,0},{4,7},{5,6},{6,5},{7,4},{8,11},{9,10},{10,... | collective-permute-start | bytes 884744 | tf_op jit(solution)/shard_map/ppermute | solution.py:681
  309.8 10.3 %collective-permute-start = (bf16[192,768]{1,0:T(8,128)(2,1)S(1)}, bf16[192,768]{1,0:T(8,128)(2,1)S(1)}, u32[]{:S(2)}, u32[]{:S(2)}) collective-permute-start(bf16[192,768]{1,0:T(8,128)(2,1)S(1)} %copy-done.15), channel_id=1, source_target_pairs={{0,1},{1,0},{2,3},{3,2},{4,5},{5,4},{6,7},{7,6},{8,9},{9,8},{10,11... | collective-permute-start | bytes 884744 | tf_op jit(solution)/shard_map/ppermute | solution.py:681
  309.8 55.8 %collective-permute-start.28 = (bf16[2,384,768]{2,1,0:T(8,128)(2,1)}, bf16[2,384,768]{2,1,0:T(8,128)(2,1)}, u32[]{:S(2)}, u32[]{:S(2)}) collective-permute-start(bf16[2,384,768]{2,1,0:T(8,128)(2,1)} %slice.117), channel_id=1, source_target_pairs={{0,16},{4,20},{8,24},{12,28},{16,0},{20,4},{24,8},{28,12},{1,17},{... | collective-permute-start | bytes 3538952 | tf_op jit(solution)/shard_map/ppermute | solution.py:681
  313.0 24.8 %collective-permute-start.2 = (bf16[192,768]{1,0:T(8,128)(2,1)S(1)}, bf16[192,768]{1,0:T(8,128)(2,1)S(1)}, u32[]{:S(2)}, u32[]{:S(2)}) collective-permute-start(bf16[192,768]{1,0:T(8,128)(2,1)S(1)} %copy-done.13), channel_id=1, source_target_pairs={{0,2},{1,3},{2,0},{3,1},{4,6},{5,7},{6,4},{7,5},{8,10},{9,11},{10,... | collective-permute-start | bytes 884744 | tf_op jit(solution)/shard_map/ppermute | solution.py:681
  320.1 19.2 %collective-permute-start.4 = (bf16[192,768]{1,0:T(8,128)(2,1)S(1)}, bf16[192,768]{1,0:T(8,128)(2,1)S(1)}, u32[]{:S(2)}, u32[]{:S(2)}) collective-permute-start(bf16[192,768]{1,0:T(8,128)(2,1)S(1)} %copy-done.11), channel_id=1, source_target_pairs={{0,3},{1,2},{2,1},{3,0},{4,7},{5,6},{6,5},{7,4},{8,11},{9,10},{10,... | collective-permute-start | bytes 884744 | tf_op jit(solution)/shard_map/ppermute | solution.py:681
  322.8 68.1 %collective-permute-start.19 = (bf16[2,768,384]{2,1,0:T(8,128)(2,1)}, bf16[2,768,384]{2,1,0:T(8,128)(2,1)}, u32[]{:S(2)}, u32[]{:S(2)}) collective-permute-start(bf16[2,768,384]{2,1,0:T(8,128)(2,1)} %slice.105), channel_id=1, source_target_pairs={{0,16},{4,20},{8,24},{12,28},{16,0},{20,4},{24,8},{28,12},{1,17},{... | collective-permute-start | bytes 3538952 | tf_op jit(solution)/shard_map/ppermute | solution.py:681
  337.8 77.6 %collective-permute-start.22 = (bf16[2,768,384]{2,1,0:T(8,128)(2,1)}, bf16[2,768,384]{2,1,0:T(8,128)(2,1)}, u32[]{:S(2)}, u32[]{:S(2)}) collective-permute-start(bf16[2,768,384]{2,1,0:T(8,128)(2,1)} %slice.109), channel_id=1, source_target_pairs={{0,16},{4,20},{8,24},{12,28},{16,0},{20,4},{24,8},{28,12},{1,17},{... | collective-permute-start | bytes 3538952 | tf_op jit(solution)/shard_map/ppermute | solution.py:681
  347.3 18.3 %copy-start.1 = (bf16[4,384,768]{2,1,0:T(8,128)(2,1)S(1)}, bf16[4,384,768]{2,1,0:T(8,128)(2,1)}, u32[]{:S(2)}) copy-start(bf16[4,384,768]{2,1,0:T(8,128)(2,1)} %copy-done) | copy-start | bytes 7077892
  347.6 43.3 %copy-start.3 = (bf16[4,768,384]{2,1,0:T(8,128)(2,1)S(1)}, bf16[4,768,384]{2,1,0:T(8,128)(2,1)}, u32[]{:S(2)}) copy-start(bf16[4,768,384]{2,1,0:T(8,128)(2,1)} %copy-done.2) | copy-start | bytes 7077892
  347.7 71.7 %collective-permute-start.26 = (bf16[1,384,768]{2,1,0:T(8,128)(2,1)S(1)}, bf16[1,384,768]{2,1,0:T(8,128)(2,1)S(1)}, u32[]{:S(2)}, u32[]{:S(2)}) collective-permute-start(bf16[1,384,768]{2,1,0:T(8,128)(2,1)S(1)} %slice.115), channel_id=1, source_target_pairs={{0,8},{4,12},{8,0},{12,4},{16,24},{20,28},{24,16},{28,20},{1,9},{5... | collective-permute-start | bytes 1769480 | tf_op jit(solution)/shard_map/ppermute | solution.py:681
  367.2 48.1 %copy-start.5 = (bf16[4,768,384]{2,1,0:T(8,128)(2,1)S(1)}, bf16[4,768,384]{2,1,0:T(8,128)(2,1)}, u32[]{:S(2)}) copy-start(bf16[4,768,384]{2,1,0:T(8,128)(2,1)} %copy-done.4) | copy-start | bytes 7077892
  367.3 52.2 %collective-permute-start.29 = (bf16[1,384,768]{2,1,0:T(8,128)(2,1)S(1)}, bf16[1,384,768]{2,1,0:T(8,128)(2,1)S(1)}, u32[]{:S(2)}, u32[]{:S(2)}) collective-permute-start(bf16[1,384,768]{2,1,0:T(8,128)(2,1)S(1)} %slice.119), channel_id=1, source_target_pairs={{0,8},{4,12},{8,0},{12,4},{16,24},{20,28},{24,16},{28,20},{1,9},{5... | collective-permute-start | bytes 1769480 | tf_op jit(solution)/shard_map/ppermute | solution.py:681
  392.6 28.0 %collective-permute-start.20 = (bf16[1,768,384]{2,1,0:T(8,128)(2,1)S(1)}, bf16[1,768,384]{2,1,0:T(8,128)(2,1)S(1)}, u32[]{:S(2)}, u32[]{:S(2)}) collective-permute-start(bf16[1,768,384]{2,1,0:T(8,128)(2,1)S(1)} %slice.107), channel_id=1, source_target_pairs={{0,8},{4,12},{8,0},{12,4},{16,24},{20,28},{24,16},{28,20},{1,9},{5... | collective-permute-start | bytes 1769480 | tf_op jit(solution)/shard_map/ppermute | solution.py:681
  417.8 14.9 %collective-permute-start.23 = (bf16[1,768,384]{2,1,0:T(8,128)(2,1)}, bf16[1,768,384]{2,1,0:T(8,128)(2,1)}, u32[]{:S(2)}, u32[]{:S(2)}) collective-permute-start(bf16[1,768,384]{2,1,0:T(8,128)(2,1)} %slice.111), channel_id=1, source_target_pairs={{0,8},{4,12},{8,0},{12,4},{16,24},{20,28},{24,16},{28,20},{1,9},{5... | collective-permute-start | bytes 1769480 | tf_op jit(solution)/shard_map/ppermute | solution.py:681
  (21 other events, 141.4 us)
Sparse Core Ops, SparseCore 0:
  278.8 80.6 reduce-scatter.1
  420.9 38.8 all-reduce.2
